TPU v7x, 32 devices: a whole 2x2x4 slice. The times are simulated.
32 devices in a mesh: row: 4 (over x, core), col: 8 (over z, y).
Axes of the slice: x: 2, y: 2, z: 4, core: 2. Of those that a mesh axis runs over, the one named last changes fastest.
Arguments:
- layer_input: bfloat16 [4224, 1024], P('col', 'row'), may hold values from -6 to 6
- w_q: bfloat16 [1024, 1024], P('col', 'row'), may hold values from -0.1875 to 0.1875
- w_k: bfloat16 [1024, 1024], P('col', 'row'), may hold values from -0.1875 to 0.1875
- w_v: bfloat16 [1024, 1024], P('col', 'row'), may hold values from -0.1875 to 0.1875
- w_o: bfloat16 [1024, 1024], P('row', 'col'), may hold values from -0.25 to 0.25
- w_gate: bfloat16 [1024, 4096], P('col', 'row'), may hold values from -0.1875 to 0.1875
- w_up: bfloat16 [1024, 4096], P('col', 'row'), may hold values from -0.1875 to 0.1875
- w_down: bfloat16 [4096, 1024], P('row', 'col'), may hold values from -0.125 to 0.125
- norm1: float32 [1024], replicated, may hold values from 0.5 to 1.5
- norm2: float32 [1024], replicated, may hold values from 0.5 to 1.5
- q_gain: float32 [1024], P('row'), may hold values from 0.5 to 1.5
- k_gain: float32 [1024], P('row'), may hold values from 0.5 to 1.5
- bias_same: float32 [16], P('row'), may hold values from -3 to 3
- bias_diff: float32 [16], P('row'), may hold values from -3 to 3
- pre_variate: int32 [8, 512], P('col'), may hold values from 0 to 7, never falling along the last dimension, each value on 1 to 128 neighbouring positions
- pre_keep: int32 [8, 512], P('col'), may hold values 0 or 1
- dec_variate: int32 [128], P('col'), may hold values from 0 to 7
- dec_len: int32 [128], P('col'), may hold values from 1 to 1023, as said below
- dec_table: int32 [128, 8], P('col'), may hold values from 0 to 31
- dec_holder: int32 [128, 1], P('col'), may hold values from 0 to 7; in each aligned block of 16 rows (0 to 15, 16 to 31, ...) at most 2 rows name the same one
- kv_pool: bfloat16 [256, 2, 128, 1024], P('col', None, None, 'row'), may hold values from -4 to 4
- page_variates: int32 [256, 128], P('col'), may hold values from 0 to 7
Outputs:
- hidden: bfloat16 [4224, 1024], P('col', 'row')
- prefill_pages: bfloat16 [32, 2, 128, 1024], P('col', None, None, 'row')
- tail_pages: bfloat16 [128, 2, 128, 1024], P('col', None, None, 'row')
Inputs may be any that keep to these rules, and one draw needn't show every extreme that they name: `pre_variate`: each variate's tokens form one run of at most 128 positions. `dec_len`: some request has exactly 1023 cached tokens. `dec_table`: entries past a request's last page are unused; requests may share pages. `dec_holder`: among the 16 requests of one column group at most 2 name the same holder, a bound that some block reaches of them.
All inputs are finite; a program needn't handle non-finite values. No bound on the sum of `pre_keep` on one device may be relied on, other than what follows from the above.
Results may differ from a plain program's by a relative error of at most 0.015.
Values may be sent and summed in bfloat16 or wider, within the bound.
A program may use at most 128 MiB of HBM per device.

v0:
```python
import jax
import jax.numpy as jnp
from jax import lax
from jax.sharding import PartitionSpec as P

HD = 64


eps = 1e-05


def as_sent(array):
    return jax.tree.map(lambda a: a.astype(jnp.bfloat16) if a.dtype == jnp.float32 else a, array)


def norm_rows(values, gain_row):
    return values * lax.rsqrt(jnp.mean(values * values, axis=-1, keepdims=True) + eps) * gain_row


def rotate(tensor, places):
    half_size = tensor.shape[-1] // 2
    spacing = jnp.arange(half_size).astype(jnp.float32) * (2.0 / tensor.shape[-1])
    angles = places.astype(jnp.float32)[:, None] * jnp.power(10000.0, -spacing)[None, :]
    cosine = jnp.cos(angles)[:, None, :]
    sine_part = jnp.sin(angles)[:, None, :]
    lower_half = tensor[..., :half_size]
    upper_half = tensor[..., half_size:]
    return jnp.concatenate(
        [
            lower_half * cosine - upper_half * sine_part,
            upper_half * cosine + lower_half * sine_part,
        ],
        axis=-1,
    )


def segment_time(variates):
    places = jnp.arange(variates.shape[0])
    run_start = jnp.concatenate([jnp.ones((1,), dtype=jnp.bool_), variates[1:] != variates[:-1]])
    starts = lax.cummax(jnp.where(run_start, places, 0), axis=0)
    return places - starts


def on_device(
    layer_input,
    w_q,
    w_k,
    w_v,
    w_o,
    w_gate,
    w_up,
    w_down,
    norm1,
    norm2,
    q_gain,
    k_gain,
    bias_same,
    bias_diff,
    pre_variate,
    pre_keep,
    dec_variate,
    dec_len,
    dec_table,
    dec_holder,
    kv_pool,
    page_variates,
):
    row_count = layer_input.shape[0]
    local_width = layer_input.shape[1]
    pre_len = pre_variate.shape[1]
    dec_count = dec_len.shape[0]
    heads_here = local_width // HD
    score_scale = HD ** (-0.5)
    page_size = kv_pool.shape[2]
    page_count = dec_table.shape[1]
    gathered_input = lax.all_gather(layer_input, "row", axis=1, tiled=True)
    normed = norm_rows(gathered_input.astype(jnp.float32), norm1).astype(jnp.bfloat16)
    pieces = (
        lax.all_gather(w_q, "col", axis=0, tiled=True),
        lax.all_gather(w_k, "col", axis=0, tiled=True),
        lax.all_gather(w_v, "col", axis=0, tiled=True),
    )
    columns = normed
    queries = jnp.dot(columns, pieces[0], preferred_element_type=jnp.float32)
    keys_proj = jnp.dot(columns, pieces[1], preferred_element_type=jnp.float32)
    values_proj = jnp.dot(columns, pieces[2], preferred_element_type=jnp.float32)
    places = jnp.concatenate([segment_time(pre_variate[0]), dec_len])
    query_rot = rotate(
        norm_rows(queries.reshape(row_count, heads_here, HD), q_gain.reshape(heads_here, HD)),
        places,
    ).astype(jnp.bfloat16)
    key_rot = rotate(
        norm_rows(keys_proj.reshape(row_count, heads_here, HD), k_gain.reshape(heads_here, HD)),
        places,
    ).astype(jnp.bfloat16)
    value_bf = values_proj.astype(jnp.bfloat16).reshape(row_count, heads_here, HD)

    def attend_slot(inputs):
        float_item, int_item = inputs
        new_query = float_item[:local_width].reshape(heads_here, HD)
        new_key = float_item[local_width : 2 * local_width]
        new_value = float_item[2 * local_width :]
        page_rows = int_item[:page_count]
        length = int_item[page_count]
        variate = int_item[page_count + 1]
        gathered = kv_pool[page_rows]
        cached_keys = gathered[:, 0].reshape(page_count * page_size, heads_here, HD)
        cached_vals = gathered[:, 1].reshape(page_count * page_size, heads_here, HD)
        key_variates = page_variates[page_rows].reshape(page_count * page_size)
        scores = (
            jnp.einsum("hd,khd->hk", new_query, cached_keys, preferred_element_type=jnp.float32)
            * score_scale
        )
        scores = scores + jnp.where(
            (key_variates == variate)[None, :], bias_same[:, None], bias_diff[:, None]
        )
        key_heads = new_key.reshape(heads_here, HD)
        value_heads = new_value.reshape(heads_here, HD)
        own_score = (
            jnp.sum(new_query.astype(jnp.float32) * key_heads.astype(jnp.float32), axis=1)
            * score_scale
            + bias_same
        )
        exp_scores = jnp.where(
            (jnp.arange(page_count * page_size) < length)[None, :], jnp.exp(scores), 0.0
        )
        own_exp = jnp.exp(own_score)
        total_weight = jnp.sum(exp_scores, axis=1) + own_exp
        weights_bf = (exp_scores / total_weight[:, None]).astype(jnp.bfloat16)
        own_weight = (own_exp / total_weight).astype(jnp.bfloat16)
        attended = jnp.einsum(
            "hk,khd->hd", weights_bf, cached_vals, preferred_element_type=jnp.float32
        ) + own_weight.astype(jnp.float32)[:, None] * value_heads.astype(jnp.float32)
        tail_slot = page_rows[length // page_size]
        old_page = kv_pool[tail_slot]
        hit_row = (jnp.arange(page_size) == length % page_size)[None, :, None]
        new_rows = jnp.stack([new_key, new_value])[:, None, :]
        return (
            attended.astype(jnp.bfloat16).reshape(local_width),
            jnp.where(hit_row, new_rows, old_page),
        )

    keep_mask = pre_keep[0]
    variates = pre_variate[0]
    block_rows = min(512, pre_len)
    pre_keys = key_rot[:pre_len]
    pre_values = value_bf[:pre_len]
    block_queries = query_rot[0:block_rows]
    scores = (
        jnp.einsum("qhd,khd->hqk", block_queries, pre_keys, preferred_element_type=jnp.float32)
        * score_scale
    )
    same_var = variates[0:block_rows, None] == variates[None, :]
    scores = scores + jnp.where(same_var[None], bias_same[:, None, None], bias_diff[:, None, None])
    allowed = (keep_mask[None, :] == 1) | (
        jnp.arange(0, block_rows)[:, None] == jnp.arange(pre_len)[None, :]
    )
    exp_scores = jnp.where(allowed[None], jnp.exp(scores), 0.0)
    weights_bf = (exp_scores / jnp.sum(exp_scores, axis=2, keepdims=True)).astype(jnp.bfloat16)
    outputs = jnp.einsum(
        "hqk,khd->qhd", weights_bf, pre_values, preferred_element_type=jnp.float32
    ).astype(jnp.bfloat16)
    prefill_out = outputs.reshape(pre_len, local_width)
    peer_count = lax.axis_size("col")
    slot_count = max(2, (dec_count + peer_count - 1) // peer_count)
    holder = dec_holder[:, 0]
    onehot = (holder[:, None] == jnp.arange(peer_count)[None, :]).astype(jnp.int32)
    slot_rank = jnp.sum((jnp.cumsum(onehot, axis=0) - onehot) * onehot, axis=1)
    target = holder * slot_count + slot_rank
    payload = jnp.concatenate(
        [
            query_rot[pre_len:].reshape(dec_count, local_width),
            key_rot[pre_len:].reshape(dec_count, local_width),
            value_bf[pre_len:].reshape(dec_count, local_width),
        ],
        axis=1,
    )
    int_facts = jnp.concatenate([dec_table, dec_len[:, None], dec_variate[:, None]], axis=1)
    send_float = (
        jnp.zeros((peer_count * slot_count, 3 * local_width), jnp.bfloat16).at[target].set(payload)
    )
    send_int = (
        jnp.zeros((peer_count * slot_count, page_count + 2), jnp.int32).at[target].set(int_facts)
    )
    send_float = send_float.reshape(peer_count, slot_count, 3 * local_width)
    send_int = send_int.reshape(peer_count, slot_count, page_count + 2)
    floats = lax.all_to_all(send_float, "col", split_axis=0, concat_axis=0, tiled=True)
    int_part = lax.all_to_all(send_int, "col", split_axis=0, concat_axis=0, tiled=True)
    group_count = floats.shape[0]
    item_count = floats.shape[1]
    flat_floats = floats.reshape(group_count * item_count, floats.shape[2])
    flat_ints = int_part.reshape(group_count * item_count, int_part.shape[2])
    batch_slots = min(16, group_count * item_count)
    slot_out, slot_tail = lax.map(attend_slot, (flat_floats, flat_ints), batch_size=batch_slots)
    slot_out = slot_out.reshape(group_count, item_count, local_width)
    slot_tail = slot_tail.reshape(group_count, item_count, 2, page_size, local_width)
    back_out = lax.all_to_all(
        as_sent(slot_out), "col", split_axis=0, concat_axis=0, tiled=True
    ).astype(slot_out.dtype)
    back_tail = lax.all_to_all(
        as_sent(slot_tail), "col", split_axis=0, concat_axis=0, tiled=True
    ).astype(slot_tail.dtype)
    decode_out = back_out.reshape(peer_count * slot_count, local_width)[target]
    tails = back_tail.reshape(peer_count * slot_count, 2, page_size, local_width)[target]
    decode_out, tail_pages = (decode_out, tails)
    all_attended = jnp.concatenate([prefill_out, decode_out], axis=0)
    partial_out = jnp.dot(
        all_attended,
        lax.all_gather(w_o, "col", axis=1, tiled=True),
        preferred_element_type=jnp.float32,
    )
    share_start = lax.axis_index("row") * local_width
    attn_total = lax.psum(partial_out.astype(jnp.bfloat16), "row").astype(jnp.float32)
    resid_full = gathered_input.astype(jnp.float32) + attn_total
    ffn_input = norm_rows(resid_full, norm2).astype(jnp.bfloat16)
    resid_share = lax.dynamic_slice_in_dim(resid_full, share_start, local_width, 1)
    zero_hidden = jnp.zeros((row_count, w_gate.shape[1]), jnp.float32)
    pieces = (
        lax.all_gather(w_gate, "col", axis=0, tiled=True),
        lax.all_gather(w_up, "col", axis=0, tiled=True),
    )
    columns = lax.slice_in_dim(ffn_input, 0, pieces[0].shape[0], axis=1)
    gate_proj = zero_hidden + jnp.dot(columns, pieces[0], preferred_element_type=jnp.float32)
    up_proj = zero_hidden + jnp.dot(columns, pieces[1], preferred_element_type=jnp.float32)
    hidden_units = (jax.nn.silu(gate_proj) * up_proj).astype(jnp.bfloat16)
    partial_ffn = jnp.dot(
        hidden_units,
        lax.all_gather(w_down, "col", axis=1, tiled=True),
        preferred_element_type=jnp.float32,
    )
    ffn_share = lax.psum_scatter(
        partial_ffn.astype(jnp.bfloat16), "row", scatter_dimension=1, tiled=True
    ).astype(jnp.float32)
    hidden = (resid_share + ffn_share).astype(jnp.bfloat16)
    prefill_pages = jnp.stack(
        [
            key_rot[:pre_len].reshape(pre_len // page_size, page_size, local_width),
            value_bf[:pre_len].reshape(pre_len // page_size, page_size, local_width),
        ],
        axis=1,
    )
    return (hidden, prefill_pages, tail_pages)


def solution(mesh):
    placed = (
        P("col", "row"),
        P("col", "row"),
        P("col", "row"),
        P("col", "row"),
        P("row", "col"),
        P("col", "row"),
        P("col", "row"),
        P("row", "col"),
        P(),
        P(),
        P("row"),
        P("row"),
        P("row"),
        P("row"),
        P("col", None),
        P("col", None),
        P("col"),
        P("col"),
        P("col", None),
        P("col", None),
        P("col", None, None, "row"),
        P("col", None),
    )
    return jax.shard_map(
        on_device,
        mesh=mesh,
        in_specs=placed,
        out_specs=(P("col", "row"), P("col", None, None, "row"), P("col", None, None, "row")),
        check_vma=False,
    )
```

profile of v0, /device:TPU:9, one launch (start us, length us, event | category | flops | bytes accessed | tf_op | source)
XLA Modules:
  0.0 471.1 jit_solution(14520708024231773946)
XLA Ops:
  13.1 5.7 %all-to-all-start = ((s32[8,2,10]{2,1,0:T(2,128)}), s32[8,2,10]{2,1,0:T(2,128)S(1)}, u32[]{:S(2)}, u32[]{:S(2)}) async-start(s32[8,2,10]{2,1,0:T(2,128)} %bitcast.13), calls=%async_computation | async-start | bytes 16384 | tf_op jit(solution)/shard_map/all_to_all | solution.py:188
  18.8 22.9 %all_gather.27 = bf16[1024,256]{1,0:T(8,128)(2,1)S(1)} all-gather(bf16[128,256]{1,0:T(8,128)(2,1)} %param.24), channel_id=1, replica_groups=mesh['row'=4,'col'=8] {'col'}, dimensions={0}, use_global_device_ids=true | all-gather | bytes 589824 | tf_op jit(solution)/shard_map/all_gather | solution.py:80
  41.7 28.0 %all_gather.26 = bf16[1024,256]{1,0:T(8,128)(2,1)} all-gather(bf16[128,256]{1,0:T(8,128)(2,1)} %param.23), channel_id=1, replica_groups=mesh['row'=4,'col'=8] {'col'}, dimensions={0}, use_global_device_ids=true | all-gather | bytes 589824 | tf_op jit(solution)/shard_map/all_gather | solution.py:79
  72.0 27.4 %all_gather.25 = bf16[1024,256]{1,0:T(8,128)(2,1)} all-gather(bf16[128,256]{1,0:T(8,128)(2,1)} %param.25), channel_id=1, replica_groups=mesh['row'=4,'col'=8] {'col'}, dimensions={0}, use_global_device_ids=true | all-gather | bytes 589824 | tf_op jit(solution)/shard_map/all_gather | solution.py:81
  99.4 24.4 %all_gather.28 = bf16[256,1024]{1,0:T(8,128)(2,1)S(1)} all-gather(bf16[256,128]{1,0:T(8,128)(2,1)S(1)} %copy-done.9), channel_id=1, replica_groups=mesh['row'=4,'col'=8] {'col'}, dimensions={1}, use_global_device_ids=true | all-gather | bytes 589824 | tf_op jit(solution)/shard_map/all_gather | solution.py:209
  125.7 10.5 %gather_fusion = bf16[128,2,128,256]{3,2,1,0:T(8,128)(2,1)} fusion(bf16[32,2,128,256]{3,2,1,0:T(8,128)(2,1)} %param.42, s32[1024]{0:T(1024)S(1)} %pad_clamp_fusion.1), kind=kCustom, calls=%fused_computation | custom fusion | bytes 33554944 | tf_op jit(solution)/shard_map/while/body/eval_jaxpr/vmap()/gather | solution.py:106
  136.2 11.7 %fusion.54 = (bf16[16,8,1,128,256]{4,3,2,1,0:T(8,128)(2,1)}, bf16[16,8,1,128,256]{4,3,2,1,0:T(8,128)(2,1)}) fusion(bf16[16,8,2,128,256]{4,3,2,1,0:T(8,128)(2,1)} %bitcast.90), kind=kLoop, calls=%fused_computation.132 | loop fusion | bytes 33554432 | tf_op jit(solution)/shard_map/while/body/eval_jaxpr/vmap()/slice | solution.py:107
  147.9 12.8 %copy.165 = bf16[16,8,1,128,256]{3,1,4,0,2:T(8,128)(2,1)} copy(bf16[16,8,1,128,256]{4,3,2,1,0:T(8,128)(2,1)} %get-tuple-element.21) | data formatting | bytes 16777216
  160.7 13.3 %squeeze.30 = bf16[16,1024,4,64]{1,3,2,0:T(8,128)(2,1)} reshape(bf16[16,8,1,128,256]{3,1,4,0,2:T(8,128)(2,1)} %copy.165) | data formatting | bytes 16777216 | tf_op jit(solution)/shard_map/while/body/eval_jaxpr/vmap()/reshape;while/body/eval_jaxpr/vmap()/squeeze | solution.py:107
  174.7 12.8 %copy.166 = bf16[16,8,1,128,256]{3,1,4,0,2:T(8,128)(2,1)} copy(bf16[16,8,1,128,256]{4,3,2,1,0:T(8,128)(2,1)} %get-tuple-element.22) | data formatting | bytes 16777216
  187.5 13.3 %squeeze.31 = bf16[16,1024,4,64]{1,3,2,0:T(8,128)(2,1)} reshape(bf16[16,8,1,128,256]{3,1,4,0,2:T(8,128)(2,1)} %copy.166) | data formatting | bytes 16777216 | tf_op jit(solution)/shard_map/while/body/eval_jaxpr/vmap()/reshape;while/body/eval_jaxpr/vmap()/squeeze | solution.py:108
  200.9 1.7 fusion.1
  202.6 2.0 multiply_reduce_fusion.1
  208.6 5.1 %all-to-all-start.1 = ((bf16[8,2,768]{2,1,0:T(2,128)(2,1)}), bf16[8,2,768]{2,1,0:T(2,128)(2,1)S(1)}, u32[]{:S(2)}, u32[]{:S(2)}) async-start(bf16[8,2,768]{2,1,0:T(2,128)(2,1)} %reshape.373), calls=%async_computation.1 | async-start | bytes 49152 | tf_op jit(solution)/shard_map/all_to_all | solution.py:187
  213.7 4.7 fusion
  219.1 4.6 fusion.57
  224.4 5.7 %fusion.18 = f32[16,4,1,64]{3,2,1,0:T(1,128)S(1)} fusion(bf16[16,1024,4,64]{1,3,2,0:T(8,128)(2,1)} %squeeze.31, bf16[16,4,1024,1]{2,0,1,3:T(8,128)(2,1)S(1)} %fusion.21), kind=kOutput, calls=%fused_computation.54 | convolution fusion | flops 8388608 | bytes 8536064 | tf_op jit(solution)/shard_map/while/body/eval_jaxpr/vmap(hk,khd->hd)/dot_general | solution.py:131
  231.0 5.5 %all-to-all-start.2 = ((bf16[8,2,256]{2,1,0:T(2,128)(2,1)}), bf16[8,2,256]{2,1,0:T(2,128)(2,1)S(1)}, u32[]{:S(2)}, u32[]{:S(2)}) async-start(bf16[8,2,256]{2,1,0:T(2,128)(2,1)} %reshape_reshape.2), calls=%async_computation.2 | async-start | bytes 16384 | tf_op jit(solution)/shard_map/all_to_all | solution.py:197
  236.4 3.9 fusion.5
  245.2 2.9 gather_fusion.3
  248.3 1.5 broadcast_select_fusion
  249.8 5.3 %all-to-all-start.3 = ((bf16[8,2,2,128,256]{4,3,2,1,0:T(8,128)(2,1)}), bf16[8,2,2,128,256]{4,3,2,1,0:T(8,128)(2,1)S(1)}, u32[]{:S(2)}, u32[]{:S(2)}) async-start(bf16[8,2,2,128,256]{4,3,2,1,0:T(8,128)(2,1)} %broadcast_select_fusion), calls=%async_computation.4 | async-start | bytes 4194304 | tf_op jit(solution)/shard_map/all_to_all | solution.py:200
  255.1 49.5 %all-reduce.2.cloned.1.call-done = bf16[528,1024]{1,0:T(8,128)(2,1)} async-done(((bf16[528,1024]{1,0:T(8,128)(2,1)}), bf16[528,1024]{1,0:T(8,128)(2,1)}) %all-reduce.2.cloned.1.call-update) | async-done | bytes 1081360 | tf_op jit(solution)/shard_map/psum | solution.py:213
  304.6 3.0 convert_add_fusion
  307.6 20.4 %all-gather.7.cloned.1.call-done = bf16[1024,1024]{1,0:T(8,128)(2,1)} async-done(((bf16[128,1024]{1,0:T(8,128)(2,1)}), bf16[1024,1024]{1,0:T(8,128)(2,1)}) %all-gather.7.cloned.1.call-update) | async-done | bytes 2097168 | tf_op jit(solution)/shard_map/all_gather | solution.py:219
  328.0 4.7 fusion.48
  332.6 46.8 %all-gather.11.cloned.1.call-done = bf16[1024,1024]{1,0:T(8,128)(2,1)} async-done(((bf16[1024,128]{1,0:T(8,128)(2,1)}), bf16[1024,1024]{1,0:T(8,128)(2,1)}) %all-gather.11.cloned.1.call-update) | async-done | bytes 2097168 | tf_op jit(solution)/shard_map/all_gather | solution.py:228
  379.5 50.9 %all-gather.9.cloned.1.call-done = bf16[1024,1024]{1,0:T(8,128)(2,1)} async-done(((bf16[128,1024]{1,0:T(8,128)(2,1)}), bf16[1024,1024]{1,0:T(8,128)(2,1)}) %all-gather.9.cloned.1.call-update) | async-done | bytes 2097168 | tf_op jit(solution)/shard_map/all_gather | solution.py:220
  430.4 6.8 %convolution_convert_fusion = bf16[528,1024]{1,0:T(8,128)(2,1)} fusion(bf16[1024,1024]{1,0:T(8,128)(2,1)} %all-gather.11.cloned.1.call-done, f32[528,1024]{1,0:T(8,128)} %fusion.48, bf16[1024,1024]{1,0:T(8,128)(2,1)} %all-gather.9.cloned.1.call-done, f32[1024]{0:T(1024)S(1)} %copy-done.21, f32[528]{0:T(1024)S(1)} %add_rsqrt_fusion.2, ...), kind=kOutput, calls=%fused_computation.22 | convolution fusion | flops 2221621248 | bytes 9607232 | tf_op jit(solution)/shard_map/dot_general | solution.py:226
  439.3 2.0 gather_fusion.4
  441.3 20.6 %reduce-scatter.2.cloned.1.call-done = bf16[528,256]{1,0:T(8,128)(2,1)} async-done(((bf16[528,1024]{1,0:T(8,128)(2,1)}), bf16[528,256]{1,0:T(8,128)(2,1)}) %reduce-scatter.2.cloned.1.call-update) | async-done | bytes 270352 | tf_op jit(solution)/shard_map/reduce_scatter | solution.py:231
  461.9 1.9 add_convert_fusion
  (137 shorter events, 23.0 us)
Async XLA Ops:
  8.0 166.0 %copy-start = (s32[32,128]{1,0:T(8,128)S(1)}, s32[32,128]{1,0:T(8,128)}, u32[]{:S(2)}) copy-start(s32[32,128]{1,0:T(8,128)} %param.43) | copy-start | bytes 49156
  8.0 116.2 %copy-start.10 = (s32[1,512]{1,0:T(1,128)S(1)}, s32[1,512]{1,0:T(1,128)}, u32[]{:S(2)}) copy-start(s32[1,512]{1,0:T(1,128)} %param.36) | copy-start | bytes 6148
  8.0 91.4 %copy-start.15 = (s32[1,512]{1,0:T(1,128)S(1)}, s32[1,512]{1,0:T(1,128)}, u32[]{:S(2)}) copy-start(s32[1,512]{1,0:T(1,128)} %param.37) | copy-start | bytes 6148
  8.0 91.4 %copy-start.9 = (bf16[256,128]{1,0:T(8,128)(2,1)S(1)}, bf16[256,128]{1,0:T(8,128)(2,1)}, u32[]{:S(2)}) copy-start(bf16[256,128]{1,0:T(8,128)(2,1)} %param.26) | copy-start | bytes 196612
  8.0 117.1 %copy-start.16 = (f32[256]{0:T(256)S(1)}, f32[256]{0:T(256)}, u32[]{:S(2)}) copy-start(f32[256]{0:T(256)} %param.33) | copy-start | bytes 3076
  8.1 117.2 %copy-start.17 = (f32[256]{0:T(256)S(1)}, f32[256]{0:T(256)}, u32[]{:S(2)}) copy-start(f32[256]{0:T(256)} %param.32) | copy-start | bytes 3076
  8.1 192.8 %all-gather.5.cloned.1.call-start = ((), (), s32[]{:S(2)}) async-start(), calls=%async_computation.5 | async-start | bytes 1351680 | tf_op jit(solution)/shard_map/all_gather | solution.py:76
  11.1 114.3 %copy-start.18 = (s32[16]{0:T(128)}, s32[16]{0:T(128)S(1)}, u32[]{:S(2)}) copy-start(s32[16]{0:T(128)S(1)} %fusion.35) | copy-start | bytes 196
  13.1 112.3 %all-to-all-start = ((s32[8,2,10]{2,1,0:T(2,128)}), s32[8,2,10]{2,1,0:T(2,128)S(1)}, u32[]{:S(2)}, u32[]{:S(2)}) async-start(s32[8,2,10]{2,1,0:T(2,128)} %bitcast.13), calls=%async_computation | async-start | bytes 16384 | tf_op jit(solution)/shard_map/all_to_all | solution.py:188
  125.1 88.6 %copy-start.6 = (pred[512,512]{0,1:T(8,128)(4,1)}, pred[512,512]{0,1:T(8,128)(4,1)S(1)}, u32[]{:S(2)}) copy-start(pred[512,512]{0,1:T(8,128)(4,1)S(1)} %get-tuple-element.65) | copy-start | bytes 786436
  125.6 75.2 %copy-start.13 = (s32[16,1]{0,1:T(1,128)}, s32[16,1]{0,1:T(1,128)S(1)}, u32[]{:S(2)}) copy-start(s32[16,1]{0,1:T(1,128)S(1)} %copy.164) | copy-start | bytes 196
  187.5 15.1 %copy-start.19 = (f32[1024]{0:T(1024)S(1)}, f32[1024]{0:T(1024)}, u32[]{:S(2)}) copy-start(f32[1024]{0:T(1024)} %param.30) | copy-start | bytes 12292
  200.9 3.7 copy-start.2
  200.9 3.7 copy-start.5
  205.7 1.0 copy-start.4
  205.7 1.0 copy-start.20
  205.9 12.5 %copy-start.3 = (bf16[512,4,64]{0,2,1:T(8,128)(2,1)}, bf16[512,4,64]{0,2,1:T(8,128)(2,1)S(1)}, u32[]{:S(2)}) copy-start(bf16[512,4,64]{0,2,1:T(8,128)(2,1)S(1)} %fusion.11) | copy-start | bytes 786436
  205.9 7.8 %copy-start.11 = (f32[4]{0:T(128)S(1)}, f32[4]{0:T(128)}, u32[]{:S(2)}) copy-start(f32[4]{0:T(128)} %param.34) | copy-start | bytes 52
  205.9 7.8 %copy-start.12 = (f32[4]{0:T(128)S(1)}, f32[4]{0:T(128)}, u32[]{:S(2)}) copy-start(f32[4]{0:T(128)} %param.35) | copy-start | bytes 52
  208.6 9.9 %all-to-all-start.1 = ((bf16[8,2,768]{2,1,0:T(2,128)(2,1)}), bf16[8,2,768]{2,1,0:T(2,128)(2,1)S(1)}, u32[]{:S(2)}, u32[]{:S(2)}) async-start(bf16[8,2,768]{2,1,0:T(2,128)(2,1)} %reshape.373), calls=%async_computation.1 | async-start | bytes 49152 | tf_op jit(solution)/shard_map/all_to_all | solution.py:187
  224.4 12.0 %copy-start.7 = (pred[512,512]{0,1:T(8,128)(4,1)S(1)}, pred[512,512]{0,1:T(8,128)(4,1)}, u32[]{:S(2)}) copy-start(pred[512,512]{0,1:T(8,128)(4,1)} %copy-done.6) | copy-start | bytes 786436
  224.4 12.0 %copy-start.8 = (pred[512,512]{0,1:T(8,128)(4,1)S(1)}, pred[512,512]{0,1:T(8,128)(4,1)}, u32[]{:S(2)}) copy-start(pred[512,512]{0,1:T(8,128)(4,1)} %get-tuple-element.66) | copy-start | bytes 786436
  231.0 9.6 %all-to-all-start.2 = ((bf16[8,2,256]{2,1,0:T(2,128)(2,1)}), bf16[8,2,256]{2,1,0:T(2,128)(2,1)S(1)}, u32[]{:S(2)}, u32[]{:S(2)}) async-start(bf16[8,2,256]{2,1,0:T(2,128)(2,1)} %reshape_reshape.2), calls=%async_computation.2 | async-start | bytes 16384 | tf_op jit(solution)/shard_map/all_to_all | solution.py:197
  236.4 68.2 %all-reduce.2.cloned.1.call-start = ((), (), s32[]{:S(2)}) async-start(), calls=%async_computation.6 | async-start | bytes 2162688 | tf_op jit(solution)/shard_map/psum | solution.py:213
  240.4 4.2 copy-start.14
  242.8 85.2 %all-gather.7.cloned.1.call-start = ((), (), s32[]{:S(2)}) async-start(), calls=%async_computation.7 | async-start | bytes 2359296 | tf_op jit(solution)/shard_map/all_gather | solution.py:219
  243.3 136.1 %all-gather.11.cloned.1.call-start = ((), (), s32[]{:S(2)}) async-start(), calls=%async_computation.9 | async-start | bytes 2359296 | tf_op jit(solution)/shard_map/all_gather | solution.py:228
  243.9 186.5 %all-gather.9.cloned.1.call-start = ((), (), s32[]{:S(2)}) async-start(), calls=%async_computation.8 | async-start | bytes 2359296 | tf_op jit(solution)/shard_map/all_gather | solution.py:220
  249.8 189.4 %all-to-all-start.3 = ((bf16[8,2,2,128,256]{4,3,2,1,0:T(8,128)(2,1)}), bf16[8,2,2,128,256]{4,3,2,1,0:T(8,128)(2,1)S(1)}, u32[]{:S(2)}, u32[]{:S(2)}) async-start(bf16[8,2,2,128,256]{4,3,2,1,0:T(8,128)(2,1)} %broadcast_select_fusion), calls=%async_computation.4 | async-start | bytes 4194304 | tf_op jit(solution)/shard_map/all_to_all | solution.py:200
  255.1 72.9 %copy-start.21 = (f32[1024]{0:T(1024)S(1)}, f32[1024]{0:T(1024)}, u32[]{:S(2)}) copy-start(f32[1024]{0:T(1024)} %param.31) | copy-start | bytes 12292
  255.1 206.8 %reduce-scatter.2.cloned.1.call-start = ((), (), s32[]{:S(2)}) async-start(), calls=%async_computation.10 | async-start | bytes 1351680 | tf_op jit(solution)/shard_map/reduce_scatter | solution.py:231
  439.3 24.5 %copy-start.1 = (s32[32,128]{1,0:T(8,128)S(1)}, s32[32,128]{1,0:T(8,128)}, u32[]{:S(2)}) copy-start(s32[32,128]{1,0:T(8,128)} %param.43) | copy-start | bytes 49156
Sparse Core Ops, SparseCore 0:
  10.5 18.5 all-gather.4
  242.9 61.6 all-reduce.1
  437.3 24.5 reduce-scatter.1
Sparse Core Ops, SparseCore 1:
  245.4 82.6 all-gather.6
  329.9 49.5 all-gather.10
  381.5 48.9 all-gather.8
where the time goes:
time: 475 us; the launch traced here: 471 us
  waiting for transfers between devices  191 us (40%)
  blocking collectives  103 us (22%)
  local copies, waits for them, and re-layouts  87.4 us (18%)
  matrix products  35.1 us (7%)
  starting transfers between devices  21.7 us (5%)
  other arithmetic  17.5 us (4%)
  between operations  15.9 us (3%)
    all_gather x1, waiting for transfers between devices, on_device(): lax.all_gather(w_up, 'col', axis=0, tiled=True)  50.9 us
    psum x1, waiting for transfers between devices, on_device(): lax.psum(partial_out.astype(jnp.bfloat16), 'row').astype(jnp.float32)  49.5 us
    all_gather x1, waiting for transfers between devices, on_device(): lax.all_gather(w_down, 'col', axis=1, tiled=True)  46.8 us
    all_gather x1, blocking collectives, on_device(): lax.all_gather(w_q, 'col', axis=0, tiled=True)  28 us
    all_gather x1, blocking collectives, on_device(): lax.all_gather(w_v, 'col', axis=0, tiled=True)  27.4 us
    unnamed x47, local copies, waits for them, and re-layouts  26.3 us
    all_gather x1, blocking collectives, on_device(): lax.all_gather(w_o, 'col', axis=1, tiled=True)  24.4 us
    all_gather x1, blocking collectives, on_device(): lax.all_gather(w_k, 'col', axis=0, tiled=True)  22.9 us
  transfers between devices with their start and end apart: 10, of which 6 were waited for; matrix products, arithmetic and copies ran while one was open for 25% of the time, Pallas kernels for 0%

commit v1 on v0

v1 whole, which is shorter than its diff:
```python
import functools

import jax
import jax.numpy as jnp
from jax import lax
from jax.experimental import pallas as pl
from jax.experimental.pallas import tpu as pltpu
from jax.sharding import PartitionSpec as P

HD = 64


eps = 1e-05


def norm_rows(values, gain_row):
    return values * lax.rsqrt(jnp.mean(values * values, axis=-1, keepdims=True) + eps) * gain_row


def rotate(tensor, places):
    half_size = tensor.shape[-1] // 2
    spacing = jnp.arange(half_size).astype(jnp.float32) * (2.0 / tensor.shape[-1])
    angles = places.astype(jnp.float32)[:, None] * jnp.power(10000.0, -spacing)[None, :]
    cosine = jnp.cos(angles)[:, None, :]
    sine_part = jnp.sin(angles)[:, None, :]
    lower_half = tensor[..., :half_size]
    upper_half = tensor[..., half_size:]
    return jnp.concatenate(
        [
            lower_half * cosine - upper_half * sine_part,
            upper_half * cosine + lower_half * sine_part,
        ],
        axis=-1,
    )


def segment_time(variates):
    places = jnp.arange(variates.shape[0])
    run_start = jnp.concatenate([jnp.ones((1,), dtype=jnp.bool_), variates[1:] != variates[:-1]])
    starts = lax.cummax(jnp.where(run_start, places, 0), axis=0)
    return places - starts


def cycle_dims(count):
    inner = 1
    while inner * inner * 4 <= count:
        inner *= 2
    return count // inner, inner


def cycle_place(member, count):
    outer, inner = cycle_dims(count)
    if inner == 1:
        return member
    z, y = member // inner, member % inner
    back = outer - 1 - z
    odd = back % 2
    along = (1 - odd) * (y - 1) + odd * (inner - 1 - y)
    return jnp.where(y == 0, z, outer + back * (inner - 1) + along)


def cycle_member(place, count):
    outer, inner = cycle_dims(count)
    if inner == 1:
        return place
    rest = jnp.maximum(place - outer, 0)
    back, along = rest // (inner - 1), rest % (inner - 1)
    odd = back % 2
    y = (1 - odd) * (1 + along) + odd * (inner - 1 - along)
    return jnp.where(place < outer, place * inner, (outer - 1 - back) * inner + y)


def gather_kernel(by_rows, n_col, n_row, *refs):
    count = len(by_rows)
    x_ref, tail_ref = refs[0], refs[1]
    shards = refs[2 : 2 + count]
    x_out, tail_out = refs[2 + count], refs[3 + count]
    wholes = refs[4 + count : 4 + 2 * count]
    own_sem, x_send, x_recv, t_send, t_recv, r_send, r_recv, l_send, l_recv = refs[4 + 2 * count :]
    me = lax.axis_index("col")
    my_row = lax.axis_index("row")
    barrier = pltpu.get_barrier_semaphore()
    for step in range(1, n_col):
        pl.semaphore_signal(
            barrier,
            inc=1,
            device_id={"col": (me + step) % n_col},
            device_id_type=pl.DeviceIdType.MESH,
        )
    for step in range(1, n_row):
        pl.semaphore_signal(
            barrier,
            inc=1,
            device_id={"row": (my_row + step) % n_row},
            device_id_type=pl.DeviceIdType.MESH,
        )
    pl.semaphore_wait(barrier, n_col + n_row - 2)

    place = cycle_place(me, n_col)
    right = cycle_member((place + 1) % n_col, n_col)
    left = cycle_member((place + n_col - 1) % n_col, n_col)
    half_way = n_col // 2

    def part(index, ref, owner, low, size):
        shard = shards[index]
        if by_rows[index]:
            depth = shard.shape[0]
            start = pl.multiple_of(owner * depth + low, 16)
            return ref.at[pl.ds(start, size)]
        width = shard.shape[1]
        if width % 128:
            return ref.at[owner, pl.ds(low, size)]
        return ref.at[pl.ds(low, size), pl.ds(pl.multiple_of(owner * width, 128), width)]

    def hop(index, step, to_right):
        shift = n_col - step if to_right else step
        owner = cycle_member((place + shift) % n_col, n_col)
        depth = shards[index].shape[0]
        low, size = 0, depth
        if step == half_way - 1:
            low, size = (0, depth // 2) if to_right else (depth // 2, depth // 2)
        there = part(index, wholes[index], owner, low, size)
        here = shards[index].at[pl.ds(low, size)] if step == 0 else there
        send, recv = (r_send, r_recv) if to_right else (l_send, l_recv)
        return pltpu.make_async_remote_copy(
            src_ref=here,
            dst_ref=there,
            send_sem=send.at[index, step],
            recv_sem=recv.at[index, step],
            device_id={"col": right if to_right else left},
            device_id_type=pl.DeviceIdType.MESH,
        )

    def x_copy(step):
        width = x_ref.shape[1]
        return pltpu.make_async_remote_copy(
            src_ref=x_ref,
            dst_ref=x_out.at[:, pl.ds(pl.multiple_of(my_row * width, 128), width)],
            send_sem=x_send.at[step],
            recv_sem=x_recv.at[step],
            device_id={"row": (my_row + step) % n_row},
            device_id_type=pl.DeviceIdType.MESH,
        )

    def t_copy(step):
        peer = (me + step) % n_col
        return pltpu.make_async_remote_copy(
            src_ref=tail_ref.at[peer],
            dst_ref=tail_out.at[me],
            send_sem=t_send.at[step],
            recv_sem=t_recv.at[step],
            device_id={"col": peer},
            device_id_type=pl.DeviceIdType.MESH,
        )

    own = [
        pltpu.make_async_copy(
            shards[i], part(i, wholes[i], me, 0, shards[i].shape[0]), own_sem.at[i]
        )
        for i in range(count)
    ]
    width = x_ref.shape[1]
    own.append(
        pltpu.make_async_copy(
            x_ref,
            x_out.at[:, pl.ds(pl.multiple_of(my_row * width, 128), width)],
            own_sem.at[count],
        )
    )
    own.append(pltpu.make_async_copy(tail_ref.at[me], tail_out.at[me], own_sem.at[count + 1]))
    for index in range(count):
        hop(index, 0, True).start()
        hop(index, 0, False).start()
    for step in range(1, n_row):
        x_copy(step).start()
    for copy in own:
        copy.start()
    for step in range(1, n_col):
        t_copy(step).start()
    for step in range(half_way):
        for index in range(count):
            for to_right in (True, False):
                hop(index, step, to_right).wait_recv()
                if step + 1 < half_way:
                    hop(index, step + 1, to_right).start()
    for step in range(half_way):
        for index in range(count):
            for to_right in (True, False):
                hop(index, step, to_right).wait_send()
    for step in range(1, n_row):
        x_copy(step).wait()
    for copy in own:
        copy.wait()
    for step in range(1, n_col):
        t_copy(step).wait()


def gather_all(layer_input, tail_send, shards, by_rows):
    n_col, n_row = lax.axis_size("col"), lax.axis_size("row")
    count = len(shards)
    half_way = n_col // 2
    shapes = [
        jax.ShapeDtypeStruct((layer_input.shape[0], layer_input.shape[1] * n_row), jnp.bfloat16),
        jax.ShapeDtypeStruct(tail_send.shape, jnp.bfloat16),
    ]
    for shard, rows in zip(shards, by_rows):
        depth, width = shard.shape
        whole = (depth * n_col, width) if rows else (depth, width * n_col)
        if not rows and width % 128:
            whole = (n_col, depth, width)
        shapes.append(jax.ShapeDtypeStruct(whole, jnp.bfloat16))
    gathered = pl.pallas_call(
        functools.partial(gather_kernel, by_rows, n_col, n_row),
        out_shape=shapes,
        in_specs=[pl.BlockSpec(memory_space=pl.ANY)] * (2 + count),
        out_specs=[pl.BlockSpec(memory_space=pl.ANY)] * (2 + count),
        scratch_shapes=[
            pltpu.SemaphoreType.DMA((count + 2,)),
            pltpu.SemaphoreType.DMA((n_row,)),
            pltpu.SemaphoreType.DMA((n_row,)),
            pltpu.SemaphoreType.DMA((n_col,)),
            pltpu.SemaphoreType.DMA((n_col,)),
            pltpu.SemaphoreType.DMA((count, half_way)),
            pltpu.SemaphoreType.DMA((count, half_way)),
            pltpu.SemaphoreType.DMA((count, half_way)),
            pltpu.SemaphoreType.DMA((count, half_way)),
        ],
        compiler_params=pltpu.CompilerParams(collective_id=0, has_side_effects=True),
        name="gather_all",
    )(layer_input, tail_send, *shards)
    return [
        jnp.swapaxes(each, 0, 1).reshape(each.shape[1], -1) if index > 1 and each.ndim == 3 else each
        for index, each in enumerate(gathered)
    ]


def on_device(
    layer_input,
    w_q,
    w_k,
    w_v,
    w_o,
    w_gate,
    w_up,
    w_down,
    norm1,
    norm2,
    q_gain,
    k_gain,
    bias_same,
    bias_diff,
    pre_variate,
    pre_keep,
    dec_variate,
    dec_len,
    dec_table,
    dec_holder,
    kv_pool,
    page_variates,
):
    row_count = layer_input.shape[0]
    local_width = layer_input.shape[1]
    pre_len = pre_variate.shape[1]
    dec_count = dec_len.shape[0]
    heads_here = local_width // HD
    score_scale = HD ** (-0.5)
    pool_pages = kv_pool.shape[0]
    page_size = kv_pool.shape[2]
    page_count = dec_table.shape[1]
    peer_count = lax.axis_size("col")
    slot_count = max(2, (dec_count + peer_count - 1) // peer_count)
    holder = dec_holder[:, 0]
    onehot = (holder[:, None] == jnp.arange(peer_count)[None, :]).astype(jnp.int32)
    slot_rank = jnp.sum((jnp.cumsum(onehot, axis=0) - onehot) * onehot, axis=1)
    target = holder * slot_count + slot_rank
    int_facts = jnp.concatenate([dec_table, dec_len[:, None], dec_variate[:, None]], axis=1)
    all_slots = peer_count * slot_count
    to_slot = target[None, :] == jnp.arange(all_slots)[:, None]
    send_int = jnp.sum(jnp.where(to_slot[:, :, None], int_facts[None], 0), axis=1)
    send_int = send_int.reshape(peer_count, slot_count, page_count + 2)
    int_part = lax.all_to_all(send_int, "col", split_axis=0, concat_axis=0, tiled=True)
    slot_ints = int_part.reshape(all_slots, page_count + 2)
    slot_table = slot_ints[:, :page_count]
    slot_len = slot_ints[:, page_count]
    slot_variate = slot_ints[:, page_count + 1]
    last_place = (slot_len // page_size)[:, None] == jnp.arange(page_count)[None, :]
    last_page = jnp.sum(jnp.where(last_place, slot_table, 0), axis=1)
    tail_send = kv_pool[last_page].reshape(peer_count, slot_count, 2, page_size, local_width)

    by_rows = (True, True, True, False, True, True, False)
    gathered_input, tail_back, full_q, full_k, full_v, full_o, full_gate, full_up, full_down = (
        gather_all(
            layer_input, tail_send, (w_q, w_k, w_v, w_o, w_gate, w_up, w_down), by_rows
        )
    )
    normed = norm_rows(gathered_input.astype(jnp.float32), norm1).astype(jnp.bfloat16)
    queries = jnp.dot(normed, full_q, preferred_element_type=jnp.float32)
    keys_proj = jnp.dot(normed, full_k, preferred_element_type=jnp.float32)
    values_proj = jnp.dot(normed, full_v, preferred_element_type=jnp.float32)
    places = jnp.concatenate([segment_time(pre_variate[0]), dec_len])
    query_rot = rotate(
        norm_rows(queries.reshape(row_count, heads_here, HD), q_gain.reshape(heads_here, HD)),
        places,
    ).astype(jnp.bfloat16)
    key_rot = rotate(
        norm_rows(keys_proj.reshape(row_count, heads_here, HD), k_gain.reshape(heads_here, HD)),
        places,
    ).astype(jnp.bfloat16)
    value_bf = values_proj.astype(jnp.bfloat16).reshape(row_count, heads_here, HD)

    payload = jnp.concatenate(
        [
            query_rot[pre_len:].reshape(dec_count, local_width),
            key_rot[pre_len:].reshape(dec_count, local_width),
            value_bf[pre_len:].reshape(dec_count, local_width),
        ],
        axis=1,
    )
    send_float = jnp.dot(
        to_slot.astype(jnp.bfloat16), payload, preferred_element_type=jnp.float32
    ).astype(jnp.bfloat16)
    floats = lax.all_to_all(
        send_float.reshape(peer_count, slot_count, 3 * local_width),
        "col",
        split_axis=0,
        concat_axis=0,
        tiled=True,
    ).reshape(all_slots, 3, heads_here, HD)

    keep_mask = pre_keep[0]
    variates = pre_variate[0]
    pre_keys = key_rot[:pre_len]
    pre_values = value_bf[:pre_len]
    scores = (
        jnp.einsum("qhd,khd->hqk", query_rot[:pre_len], pre_keys, preferred_element_type=jnp.float32)
        * score_scale
    )
    same_var = variates[:, None] == variates[None, :]
    scores = scores + jnp.where(same_var[None], bias_same[:, None, None], bias_diff[:, None, None])
    allowed = (keep_mask[None, :] == 1) | (
        jnp.arange(pre_len)[:, None] == jnp.arange(pre_len)[None, :]
    )
    exp_scores = jnp.where(allowed[None], jnp.exp(scores), 0.0)
    weights_bf = (exp_scores / jnp.sum(exp_scores, axis=2, keepdims=True)).astype(jnp.bfloat16)
    outputs = jnp.einsum(
        "hqk,khd->qhd", weights_bf, pre_values, preferred_element_type=jnp.float32
    ).astype(jnp.bfloat16)
    prefill_out = outputs.reshape(pre_len, local_width)

    new_query, new_key, new_value = floats[:, 0], floats[:, 1], floats[:, 2]
    head_eye = jnp.eye(heads_here, dtype=jnp.bfloat16)
    spread = (new_query[:, :, None, :] * head_eye[None, :, :, None]).reshape(
        all_slots * heads_here, local_width
    )
    pool_keys = kv_pool[:, 0].reshape(pool_pages * page_size, local_width)
    pool_vals = kv_pool[:, 1].reshape(pool_pages * page_size, local_width)
    dec_scores = (
        lax.dot_general(
            spread, pool_keys, (((1,), (1,)), ((), ())), preferred_element_type=jnp.float32
        )
        * score_scale
    ).reshape(all_slots, heads_here, pool_pages * page_size)
    pool_page = jnp.arange(pool_pages * page_size) // page_size
    pool_row = jnp.arange(pool_pages * page_size) % page_size
    times_used = jnp.zeros((all_slots, pool_pages * page_size), jnp.float32)
    for entry in range(page_count):
        left_over = (slot_len - entry * page_size)[:, None]
        hit = (slot_table[:, entry][:, None] == pool_page[None]) & (pool_row[None] < left_over)
        times_used = times_used + hit.astype(jnp.float32)
    same_dec = page_variates.reshape(1, -1) == slot_variate[:, None]
    dec_scores = dec_scores + jnp.where(
        same_dec[:, None], bias_same[None, :, None], bias_diff[None, :, None]
    )
    dec_exp = jnp.where(
        times_used[:, None] > 0, jnp.exp(dec_scores) * times_used[:, None], 0.0
    )
    own_score = (
        jnp.sum(new_query.astype(jnp.float32) * new_key.astype(jnp.float32), axis=2) * score_scale
        + bias_same[None]
    )
    own_exp = jnp.exp(own_score)
    total_weight = jnp.sum(dec_exp, axis=2) + own_exp
    dec_weights = (dec_exp / total_weight[:, :, None]).astype(jnp.bfloat16)
    own_weight = (own_exp / total_weight).astype(jnp.bfloat16)
    mixed = jnp.dot(
        dec_weights.reshape(all_slots * heads_here, pool_pages * page_size),
        pool_vals,
        preferred_element_type=jnp.float32,
    ).reshape(all_slots, heads_here, heads_here, HD)
    attended = jnp.sum(mixed * jnp.eye(heads_here)[None, :, :, None], axis=1) + own_weight.astype(
        jnp.float32
    )[:, :, None] * new_value.astype(jnp.float32)
    back_out = lax.all_to_all(
        attended.astype(jnp.bfloat16).reshape(peer_count, slot_count, local_width),
        "col",
        split_axis=0,
        concat_axis=0,
        tiled=True,
    )
    decode_out = jnp.dot(
        to_slot.T.astype(jnp.bfloat16),
        back_out.reshape(all_slots, local_width),
        preferred_element_type=jnp.float32,
    ).astype(jnp.bfloat16)
    old_tails = tail_back.reshape(all_slots, 2, page_size, local_width)[target]
    hit_row = (jnp.arange(page_size)[None, :] == (dec_len % page_size)[:, None])[:, None, :, None]
    new_rows = payload[:, local_width:].reshape(dec_count, 2, 1, local_width)
    tail_pages = jnp.where(hit_row, new_rows, old_tails)

    all_attended = jnp.concatenate([prefill_out, decode_out], axis=0)
    partial_out = jnp.dot(all_attended, full_o, preferred_element_type=jnp.float32)
    share_start = lax.axis_index("row") * local_width
    attn_total = lax.psum(partial_out.astype(jnp.bfloat16), "row").astype(jnp.float32)
    resid_full = gathered_input.astype(jnp.float32) + attn_total
    ffn_input = norm_rows(resid_full, norm2).astype(jnp.bfloat16)
    resid_share = lax.dynamic_slice_in_dim(resid_full, share_start, local_width, 1)
    gate_proj = jnp.dot(ffn_input, full_gate, preferred_element_type=jnp.float32)
    up_proj = jnp.dot(ffn_input, full_up, preferred_element_type=jnp.float32)
    hidden_units = (jax.nn.silu(gate_proj) * up_proj).astype(jnp.bfloat16)
    partial_ffn = jnp.dot(hidden_units, full_down, preferred_element_type=jnp.float32)
    ffn_share = lax.psum_scatter(
        partial_ffn.astype(jnp.bfloat16), "row", scatter_dimension=1, tiled=True
    ).astype(jnp.float32)
    hidden = (resid_share + ffn_share).astype(jnp.bfloat16)
    prefill_pages = jnp.stack(
        [
            key_rot[:pre_len].reshape(pre_len // page_size, page_size, local_width),
            value_bf[:pre_len].reshape(pre_len // page_size, page_size, local_width),
        ],
        axis=1,
    )
    return (hidden, prefill_pages, tail_pages)


def solution(mesh):
    placed = (
        P("col", "row"),
        P("col", "row"),
        P("col", "row"),
        P("col", "row"),
        P("row", "col"),
        P("col", "row"),
        P("col", "row"),
        P("row", "col"),
        P(),
        P(),
        P("row"),
        P("row"),
        P("row"),
        P("row"),
        P("col", None),
        P("col", None),
        P("col"),
        P("col"),
        P("col", None),
        P("col", None),
        P("col", None, None, "row"),
        P("col", None),
    )
    return jax.shard_map(
        on_device,
        mesh=mesh,
        in_specs=placed,
        out_specs=(P("col", "row"), P("col", None, None, "row"), P("col", None, None, "row")),
        check_vma=False,
    )
```

time: 475 us -> 325 us (0.68)
  waiting for transfers between devices: 191 us -> 58.8 us
  Pallas kernels: 0 us -> 129 us
  blocking collectives: 103 us -> 0 us
  local copies, waits for them, and re-layouts: 87.4 us -> 42.1 us
  other arithmetic: 17.5 us -> 29.8 us
  starting transfers between devices: 21.7 us -> 15.9 us
    pallas_call x0 -> x1, Pallas kernels: none -> 129 us  [gather_all(): pl.pallas_call(functools.partial(gather_kernel, by_rows, n_col, n_row), o...]
    all_gather x4 -> x0, waiting for transfers between devices: 118 us -> none  [the longest x1 50.9 us: on_device(): lax.all_gather(w_up, 'col', axis=0, tiled=True)]
    all_gather x4 -> x0, blocking collectives: 103 us -> none  [the longest x1 28 us: on_device(): lax.all_gather(w_q, 'col', axis=0, tiled=True)]
    squeeze x3 -> x0, local copies, waits for them, and re-layouts: 26.6 us -> none  [the longest x1 13.3 us: attend_slot(): cached_keys = gathered[:, 0].reshape(page_count * page_size, heads_here, HD)]
    unnamed x47 -> x67, local copies, waits for them, and re-layouts: 26.3 us -> 1.58 us
    psum x1, waiting for transfers between devices: 49.5 us -> 37.8 us  [on_device(): lax.psum(partial_out.astype(jnp.bfloat16), 'row').astype(jnp.float32)]
    gather x7 -> x2, local copies, waits for them, and re-layouts: 17.4 us -> 6.46 us  [the longest x1 4.19 us: on_device(): kv_pool[last_page]]
    broadcast_in_dim x2 -> x8, local copies, waits for them, and re-layouts: 0.1 us -> 8.85 us  [the longest x6 5.05 us: on_device(): jnp.where(same_dec[:, None], bias_same[None, :, None], bias_diff[None, :,...]
  transfers between devices with their start and end apart: 10 -> 5, of which waited for: 6 -> 2; matrix products, arithmetic and copies ran while one was open for 25% -> 15% of each run, Pallas kernels for 0% -> 0%
where the time goes in v1:
time: 325 us; the launch traced here: 322 us
  Pallas kernels  129 us (40%)
  waiting for transfers between devices  58.8 us (18%)
  local copies, waits for them, and re-layouts  42.1 us (13%)
  matrix products  32.2 us (10%)
  other arithmetic  29.8 us (9%)
  starting transfers between devices  15.9 us (5%)
  between operations  14.6 us (4%)
    pallas_call x1, Pallas kernels, gather_all(): pl.pallas_call(functools.partial(gather_kernel, by_rows, n_col, n_row), o...  129 us
    psum x1, waiting for transfers between devices, on_device(): lax.psum(partial_out.astype(jnp.bfloat16), 'row').astype(jnp.float32)  37.8 us
    reduce_scatter x1, waiting for transfers between devices, on_device(): lax.psum_scatter(partial_ffn.astype(jnp.bfloat16), 'row', scatter_dimensi...  20.9 us
  transfers between devices with their start and end apart: 5, of which 2 were waited for; matrix products, arithmetic and copies ran while one was open for 15% of the time, Pallas kernels for 0%

profile of v1, /device:TPU:9, one launch (start us, length us, event | category | flops | bytes accessed | tf_op | source)
XLA Modules:
  0.0 322.2 jit_solution(17248395552232047078)
XLA Ops:
  11.7 5.7 %all-to-all-start = ((s32[8,2,10]{2,1,0:T(2,128)}), s32[8,2,10]{2,1,0:T(2,128)S(1)}, u32[]{:S(2)}, u32[]{:S(2)}) async-start(s32[8,2,10]{2,1,0:T(2,128)} %bitcast.3), calls=%async_computation | async-start | bytes 16384 | tf_op jit(solution)/shard_map/all_to_all | solution.py:281
  21.0 4.0 %fusion.59 = (bf16[32,1,128,256]{3,2,1,0:T(8,128)(2,1)S(1)}, bf16[32,1,128,256]{3,2,1,0:T(8,128)(2,1)}) fusion(bf16[32,2,128,256]{3,2,1,0:T(8,128)(2,1)} %param.42), kind=kLoop, calls=%fused_computation.162 | loop fusion | bytes 8388608 | tf_op jit(solution)/shard_map/slice | solution.py:355
  29.0 4.1 %copy.184 = bf16[4096,256]{0,1:T(8,128)(2,1)} copy(bf16[4096,256]{1,0:T(8,128)(2,1)} %bitcast.105) | data formatting | bytes 4194304 | tf_op jit(solution)/shard_map/reshape;squeeze | solution.py:356
  34.9 4.2 %gather_fusion = bf16[16,2,128,256]{3,2,1,0:T(8,128)(2,1)} fusion(bf16[32,2,128,256]{3,2,1,0:T(8,128)(2,1)} %param.42, s32[1024]{0:T(1024)S(1)} %pad_clamp_fusion.1), kind=kCustom, calls=%fused_computation | custom fusion | bytes 4194368 | tf_op jit(solution)/shard_map/gather | solution.py:288
  39.1 128.8 %gather_all.1 = (bf16[528,1024]{1,0:T(8,128)(2,1)}, bf16[8,2,2,128,256]{4,3,2,1,0:T(8,128)(2,1)}, bf16[1024,256]{1,0:T(8,128)(2,1)}, bf16[1024,256]{1,0:T(8,128)...) custom-call(bf16[528,256]{1,0:T(8,128)(2,1)} %refs_0_.1, ...), custom_call_target="tpu_custom_call" | custom-call | tf_op jit(solution)/shard_map/gather_all/pallas_call | solution.py:212
  167.9 1.7 fusion.5
  169.6 2.1 multiply_reduce_fusion.1
  175.3 1.5 copy.197
  177.4 1.5 convolution_convert_fusion.3
  180.3 4.5 %all-to-all-start.1 = ((bf16[8,2,768]{2,1,0:T(2,128)(2,1)}), bf16[8,2,768]{2,1,0:T(2,128)(2,1)}, u32[]{:S(2)}, u32[]{:S(2)}) async-start(bf16[8,2,768]{2,1,0:T(2,128)(2,1)} %reshape.1235), calls=%async_computation.1 | async-start | bytes 49152 | tf_op jit(solution)/shard_map/all_to_all | solution.py:322
  186.2 1.9 broadcast_compare_fusion.2
  188.1 5.6 %fusion.4 = (f32[4,512]{1,0:T(4,128)}, f32[4,512,512]{1,2,0:T(8,128)}) fusion(f32[4]{0:T(128)} %param.35, f32[4]{0:T(128)} %param.34, pred[512,512]{0,1:T(8,128)(4,1)} %get-tuple-element.72, pred[512,512]{0,1:T(8,128)(4,1)} %get-tuple-element.71, bf16[512,4,64]{0,2,1:T(8,128)(2,1)S(1)} %fusion.17, bf16[528,4,32]{0,2,1:T(8,128)(2,1)} %copy-done.5, ...), kind=kOutput, calls=%fused_computation.12 | convolution fusion | flops 139982848 | bytes 5259296 | tf_op jit(solution)/shard_map/qhd,khd->hqk/dot_general | solution.py:335
  194.5 2.2 mul.319
  196.7 2.6 mul.320
  199.2 1.8 broadcast_in_dim.135
  201.1 2.0 broadcast_in_dim.136
  203.0 1.8 broadcast_in_dim.137
  204.9 2.0 broadcast_in_dim.138
  211.4 3.2 %fusion.60 = (f32[64]{0:T(128)S(1)}, f32[64,4096]{1,0:T(8,128)}) fusion(pred[64,4096]{1,0:T(32,128)(4,1)} %broadcast_in_dim.136, f32[64,4096]{1,0:T(8,128)} %mul.320, pred[64,4096]{1,0:T(32,128)(4,1)} %broadcast_in_dim.138, f32[64]{0:T(128)} %broadcast_in_dim.149, f32[64]{0:T(128)} %broadcast_in_dim.140, bf16[64,256]{1,0:T(8,128)(2,1)S(1)} %mul.316, ...), kind=kOutput, calls=%fused_computation.163 | convolution fusion | flops 135790528 | bytes 4752128 | tf_op jit(solution)/shard_map/dot_general | solution.py:358
  216.7 2.2 divide_convert_fusion.4
  218.8 2.0 dot_general.52
  220.9 2.2 fusion.10
  224.1 5.4 %all-to-all-start.2 = ((bf16[8,2,256]{2,1,0:T(2,128)(2,1)}), bf16[8,2,256]{2,1,0:T(2,128)(2,1)S(1)}, u32[]{:S(2)}, u32[]{:S(2)}) async-start(bf16[8,2,256]{2,1,0:T(2,128)(2,1)} %add_convert_fusion.3), calls=%async_computation.2 | async-start | bytes 16384 | tf_op jit(solution)/shard_map/all_to_all | solution.py:393
  229.6 4.2 %fusion.9 = bf16[4,64,512]{2,1,0:T(8,128)(2,1)S(1)} fusion(bf16[512,4,64]{0,2,1:T(8,128)(2,1)} %bitcast.115, f32[4,512,512]{1,2,0:T(8,128)} %get-tuple-element.66, f32[4,512]{1,0:T(4,128)} %get-tuple-element.65, f32[4]{0:T(128)S(1)} %copy-done.26, f32[4]{0:T(128)S(1)} %copy-done.16, pred[512,512]{0,1:T(8,128)(4,1)} %get-tuple-element.72, ...), kind=kOutput, calls=%fused_computation.24 | convolution fusion | flops 140640256 | bytes 5251104 | tf_op jit(solution)/shard_map/hqk,khd->qhd/dot_general | solution.py:345
  235.8 37.8 %all-reduce.2.cloned.1.call-done = bf16[528,1024]{1,0:T(8,128)(2,1)} async-done(((bf16[528,1024]{1,0:T(8,128)(2,1)}), bf16[528,1024]{1,0:T(8,128)(2,1)}) %all-reduce.2.cloned.1.call-update) | async-done | bytes 1081360 | tf_op jit(solution)/shard_map/psum | solution.py:413
  273.7 3.0 convert_add_fusion
  276.7 4.3 %fusion.53 = f32[528,1024]{1,0:T(8,128)} fusion(bf16[1024,1024]{1,0:T(8,128)(2,1)} %get-tuple-element.17, f32[1024]{0:T(1024)S(1)} %copy-done.32, f32[528]{0:T(1024)S(1)} %add_rsqrt_fusion.2, bf16[528,1024]{1,0:T(8,128)(2,1)S(1)} %copy-done, bf16[528,1024]{1,0:T(8,128)(2,1)S(1)} %copy-done.2), kind=kOutput, calls=%fused_computation.159 | convolution fusion | flops 1110540288 | bytes 6428736 | tf_op jit(solution)/shard_map/dot_general | solution.py:417
  281.0 6.4 %convolution_convert_fusion = bf16[528,1024]{1,0:T(8,128)(2,1)} fusion(bf16[1024,1024]{1,0:T(8,128)(2,1)} %get-tuple-element.19, f32[528,1024]{1,0:T(8,128)} %fusion.53, bf16[1024,1024]{1,0:T(8,128)(2,1)} %get-tuple-element.18, f32[1024]{0:T(1024)S(1)} %copy-done.32, f32[528]{0:T(1024)S(1)} %add_rsqrt_fusion.2, bf16[528,1024]{1,0:T(8,128)(2,1)S(1)} %copy-done, ...), kind=kOutput, calls=%fused_computation.21 | convolution fusion | flops 2221621248 | bytes 9607232 | tf_op jit(solution)/shard_map/dot_general | solution.py:420
  287.9 2.3 gather_fusion.1
  291.0 1.5 broadcast_select_fusion
  292.5 20.9 %reduce-scatter.2.cloned.1.call-done = bf16[528,256]{1,0:T(8,128)(2,1)} async-done(((bf16[528,1024]{1,0:T(8,128)(2,1)}), bf16[528,256]{1,0:T(8,128)(2,1)}) %reduce-scatter.2.cloned.1.call-update) | async-done | bytes 270352 | tf_op jit(solution)/shard_map/reduce_scatter | solution.py:421
  313.4 1.9 add_convert_fusion
  (156 shorter events, 32.5 us)
Async XLA Ops:
  11.7 21.5 %all-to-all-start = ((s32[8,2,10]{2,1,0:T(2,128)}), s32[8,2,10]{2,1,0:T(2,128)S(1)}, u32[]{:S(2)}, u32[]{:S(2)}) async-start(s32[8,2,10]{2,1,0:T(2,128)} %bitcast.3), calls=%async_computation | async-start | bytes 16384 | tf_op jit(solution)/shard_map/all_to_all | solution.py:281
  20.9 4.4 %copy-start.11 = (s32[1,512]{1,0:T(1,128)S(1)}, s32[1,512]{1,0:T(1,128)}, u32[]{:S(2)}) copy-start(s32[1,512]{1,0:T(1,128)} %param.36) | copy-start | bytes 6148
  20.9 6.1 %copy-start.23 = (f32[256]{0:T(256)S(1)}, f32[256]{0:T(256)}, u32[]{:S(2)}) copy-start(f32[256]{0:T(256)} %param.33) | copy-start | bytes 3076
  20.9 6.1 %copy-start.24 = (f32[256]{0:T(256)S(1)}, f32[256]{0:T(256)}, u32[]{:S(2)}) copy-start(f32[256]{0:T(256)} %param.32) | copy-start | bytes 3076
  21.0 6.2 %copy-start.15 = (f32[4]{0:T(128)S(1)}, f32[4]{0:T(128)}, u32[]{:S(2)}) copy-start(f32[4]{0:T(128)} %param.34) | copy-start | bytes 52
  21.0 6.8 %copy-start.25 = (f32[4]{0:T(128)S(1)}, f32[4]{0:T(128)}, u32[]{:S(2)}) copy-start(f32[4]{0:T(128)} %param.35) | copy-start | bytes 52
  34.1 133.8 %copy-start.17 = (s32[16,1]{0,1:T(1,128)}, s32[16,1]{0,1:T(1,128)S(1)}, u32[]{:S(2)}) copy-start(s32[16,1]{0,1:T(1,128)S(1)} %copy.202) | copy-start | bytes 196
  39.1 130.5 %copy-start.31 = (f32[1024]{0:T(1024)S(1)}, f32[1024]{0:T(1024)}, u32[]{:S(2)}) copy-start(f32[1024]{0:T(1024)} %param.30) | copy-start | bytes 12292
  167.9 3.8 %copy-start = (bf16[528,1024]{1,0:T(8,128)(2,1)S(1)}, bf16[528,1024]{1,0:T(8,128)(2,1)}, u32[]{:S(2)}) copy-start(bf16[528,1024]{1,0:T(8,128)(2,1)} %get-tuple-element.12) | copy-start | bytes 3244036
  167.9 3.8 %copy-start.30 = (bf16[1024,256]{1,0:T(8,128)(2,1)S(1)}, bf16[1024,256]{1,0:T(8,128)(2,1)}, u32[]{:S(2)}) copy-start(bf16[1024,256]{1,0:T(8,128)(2,1)} %get-tuple-element.14) | copy-start | bytes 1572868
  171.7 1.0 copy-start.29
  174.2 10.6 %copy-start.14 = (s32[32,128]{1,0:T(8,128)S(1)}, s32[32,128]{1,0:T(8,128)}, u32[]{:S(2)}) copy-start(s32[32,128]{1,0:T(8,128)} %param.43) | copy-start | bytes 49156
  174.4 13.6 %copy-start.3 = (bf16[512,4,64]{0,2,1:T(8,128)(2,1)}, bf16[512,4,64]{0,2,1:T(8,128)(2,1)S(1)}, u32[]{:S(2)}) copy-start(bf16[512,4,64]{0,2,1:T(8,128)(2,1)S(1)} %fusion.17) | copy-start | bytes 786436
  180.3 26.6 %all-to-all-start.1 = ((bf16[8,2,768]{2,1,0:T(2,128)(2,1)}), bf16[8,2,768]{2,1,0:T(2,128)(2,1)}, u32[]{:S(2)}, u32[]{:S(2)}) async-start(bf16[8,2,768]{2,1,0:T(2,128)(2,1)} %reshape.1235), calls=%async_computation.1 | async-start | bytes 49152 | tf_op jit(solution)/shard_map/all_to_all | solution.py:322
  188.1 5.6 %copy-start.9 = (bf16[528,256]{1,0:T(8,128)(2,1)S(1)}, bf16[528,256]{1,0:T(8,128)(2,1)}, u32[]{:S(2)}) copy-start(bf16[528,256]{1,0:T(8,128)(2,1)} %copy-done.8) | copy-start | bytes 811012
  211.3 3.9 %copy-start.13 = (f32[16,4]{1,0:T(8,128)S(1)}, f32[16,4]{1,0:T(8,128)}, u32[]{:S(2)}) copy-start(f32[16,4]{1,0:T(8,128)} %fusion.21) | copy-start | bytes 772
  214.6 6.3 %copy-start.1 = (bf16[4096,256]{0,1:T(8,128)(2,1)S(1)}, bf16[4096,256]{0,1:T(8,128)(2,1)}, u32[]{:S(2)}) copy-start(bf16[4096,256]{0,1:T(8,128)(2,1)} %copy.184) | copy-start | bytes 6291460
  220.9 2.5 copy-start.10
  220.9 8.7 %copy-start.16 = (f32[4]{0:T(128)S(1)}, f32[4]{0:T(128)}, u32[]{:S(2)}) copy-start(f32[4]{0:T(128)} %param.34) | copy-start | bytes 52
  220.9 8.7 %copy-start.26 = (f32[4]{0:T(128)S(1)}, f32[4]{0:T(128)}, u32[]{:S(2)}) copy-start(f32[4]{0:T(128)} %param.35) | copy-start | bytes 52
  224.1 9.6 %all-to-all-start.2 = ((bf16[8,2,256]{2,1,0:T(2,128)(2,1)}), bf16[8,2,256]{2,1,0:T(2,128)(2,1)S(1)}, u32[]{:S(2)}, u32[]{:S(2)}) async-start(bf16[8,2,256]{2,1,0:T(2,128)(2,1)} %add_convert_fusion.3), calls=%async_computation.2 | async-start | bytes 16384 | tf_op jit(solution)/shard_map/all_to_all | solution.py:393
  229.5 44.2 %all-reduce.2.cloned.1.call-start = ((), (), s32[]{:S(2)}) async-start(), calls=%async_computation.4 | async-start | bytes 2162688 | tf_op jit(solution)/shard_map/psum | solution.py:413
  229.5 4.2 %copy-start.21 = (s32[16]{0:T(128)S(1)}, s32[16]{0:T(128)}, u32[]{:S(2)}) copy-start(s32[16]{0:T(128)} %copy-done.20) | copy-start | bytes 196
  229.6 4.5 %copy-start.7 = (bf16[256,1024]{1,0:T(8,128)(2,1)S(1)}, bf16[256,1024]{1,0:T(8,128)(2,1)}, u32[]{:S(2)}) copy-start(bf16[256,1024]{1,0:T(8,128)(2,1)} %get-tuple-element.16) | copy-start | bytes 1572868
  235.6 41.1 %copy-start.32 = (f32[1024]{0:T(1024)S(1)}, f32[1024]{0:T(1024)}, u32[]{:S(2)}) copy-start(f32[1024]{0:T(1024)} %param.31) | copy-start | bytes 12292
  235.6 77.9 %reduce-scatter.2.cloned.1.call-start = ((), (), s32[]{:S(2)}) async-start(), calls=%async_computation.5 | async-start | bytes 1351680 | tf_op jit(solution)/shard_map/reduce_scatter | solution.py:421
  273.7 3.0 copy-start.2
  281.0 6.4 %copy-start.19 = (s32[16,1]{0,1:T(1,128)S(1)}, s32[16,1]{0,1:T(1,128)}, u32[]{:S(2)}) copy-start(s32[16,1]{0,1:T(1,128)} %param.41) | copy-start | bytes 196
  281.0 6.4 %copy-start.28 = (s32[16]{0:T(128)S(1)}, s32[16]{0:T(128)}, u32[]{:S(2)}) copy-start(s32[16]{0:T(128)} %copy-done.27) | copy-start | bytes 196
  281.0 6.5 %copy-start.22 = (s32[16]{0:T(128)S(1)}, s32[16]{0:T(128)}, u32[]{:S(2)}) copy-start(s32[16]{0:T(128)} %param.39) | copy-start | bytes 196
  281.0 6.6 %copy-start.4 = (bf16[512,4,64]{0,2,1:T(8,128)(2,1)S(1)}, bf16[512,4,64]{0,2,1:T(8,128)(2,1)}, u32[]{:S(2)}) copy-start(bf16[512,4,64]{0,2,1:T(8,128)(2,1)} %copy-done.3) | copy-start | bytes 786436
  281.0 6.7 %copy-start.12 = (bf16[16,1,256]{2,0,1:T(8,128)(2,1)S(1)}, bf16[16,1,256]{2,0,1:T(8,128)(2,1)}, u32[]{:S(2)}) copy-start(bf16[16,1,256]{2,0,1:T(8,128)(2,1)} %get-tuple-element.40) | copy-start | bytes 24580
  (6 other events, 4.2 us)
Sparse Core Ops, SparseCore 0:
  235.7 37.9 all-reduce.1
  287.5 25.8 reduce-scatter.1

commit v2 on v1

v2 whole, which is shorter than its diff:
```python
import functools

import jax
import jax.numpy as jnp
from jax import lax
from jax.experimental import pallas as pl
from jax.experimental.pallas import tpu as pltpu
from jax.sharding import PartitionSpec as P

HD = 64


eps = 1e-05


def norm_rows(values, gain_row):
    return values * lax.rsqrt(jnp.mean(values * values, axis=-1, keepdims=True) + eps) * gain_row


def rotate(tensor, places):
    half_size = tensor.shape[-1] // 2
    spacing = jnp.arange(half_size).astype(jnp.float32) * (2.0 / tensor.shape[-1])
    angles = places.astype(jnp.float32)[:, None] * jnp.power(10000.0, -spacing)[None, :]
    cosine = jnp.cos(angles)[:, None, :]
    sine_part = jnp.sin(angles)[:, None, :]
    lower_half = tensor[..., :half_size]
    upper_half = tensor[..., half_size:]
    return jnp.concatenate(
        [
            lower_half * cosine - upper_half * sine_part,
            upper_half * cosine + lower_half * sine_part,
        ],
        axis=-1,
    )


def segment_time(variates):
    places = jnp.arange(variates.shape[0])
    run_start = jnp.concatenate([jnp.ones((1,), dtype=jnp.bool_), variates[1:] != variates[:-1]])
    starts = lax.cummax(jnp.where(run_start, places, 0), axis=0)
    return places - starts


def cycle_dims(count):
    inner = 1
    while inner * inner * 4 <= count:
        inner *= 2
    return count // inner, inner


def cycle_place(member, count):
    outer, inner = cycle_dims(count)
    if inner == 1:
        return member
    z, y = member // inner, member % inner
    back = outer - 1 - z
    odd = back % 2
    along = (1 - odd) * (y - 1) + odd * (inner - 1 - y)
    return jnp.where(y == 0, z, outer + back * (inner - 1) + along)


def cycle_member(place, count):
    outer, inner = cycle_dims(count)
    if inner == 1:
        return place
    rest = jnp.maximum(place - outer, 0)
    back, along = rest // (inner - 1), rest % (inner - 1)
    odd = back % 2
    y = (1 - odd) * (1 + along) + odd * (inner - 1 - along)
    return jnp.where(place < outer, place * inner, (outer - 1 - back) * inner + y)


def greet(n_col, n_row):
    me, my_row = lax.axis_index("col"), lax.axis_index("row")
    barrier = pltpu.get_barrier_semaphore()
    for step in range(1, n_col):
        pl.semaphore_signal(
            barrier,
            inc=1,
            device_id={"col": (me + step) % n_col},
            device_id_type=pl.DeviceIdType.MESH,
        )
    for step in range(1, n_row):
        pl.semaphore_signal(
            barrier,
            inc=1,
            device_id={"row": (my_row + step) % n_row},
            device_id_type=pl.DeviceIdType.MESH,
        )
    pl.semaphore_wait(barrier, n_col + n_row - 2)


def ring_hops(by_rows, n_col, shards, wholes, sems):
    me = lax.axis_index("col")
    place = cycle_place(me, n_col)
    right = cycle_member((place + 1) % n_col, n_col)
    left = cycle_member((place + n_col - 1) % n_col, n_col)
    half_way = n_col // 2
    r_send, r_recv, l_send, l_recv = sems

    def part(index, owner, low, size):
        shard, ref = shards[index], wholes[index]
        if by_rows[index]:
            depth = shard.shape[0]
            start = pl.multiple_of(owner * depth + low, 16)
            return ref.at[pl.ds(start, size)]
        width = shard.shape[1]
        if width % 128:
            return ref.at[owner, pl.ds(low, size)]
        return ref.at[pl.ds(low, size), pl.ds(pl.multiple_of(owner * width, 128), width)]

    def hop(index, step, to_right):
        shift = n_col - step if to_right else step
        owner = cycle_member((place + shift) % n_col, n_col)
        depth = shards[index].shape[0]
        low, size = 0, depth
        if step == half_way - 1:
            low, size = (0, depth // 2) if to_right else (depth // 2, depth // 2)
        there = part(index, owner, low, size)
        here = shards[index].at[pl.ds(low, size)] if step == 0 else there
        send, recv = (r_send, r_recv) if to_right else (l_send, l_recv)
        return pltpu.make_async_remote_copy(
            src_ref=here,
            dst_ref=there,
            send_sem=send.at[index, step],
            recv_sem=recv.at[index, step],
            device_id={"col": right if to_right else left},
            device_id_type=pl.DeviceIdType.MESH,
        )

    def own_copy(index, sem):
        return pltpu.make_async_copy(
            shards[index], part(index, me, 0, shards[index].shape[0]), sem
        )

    return hop, own_copy


def whole_shape(shard, rows, n_col):
    depth, width = shard.shape
    if rows:
        return (depth * n_col, width)
    if width % 128:
        return (n_col, depth, width)
    return (depth, width * n_col)


def gather_kernel(by_rows, n_col, n_row, *refs):
    count = len(by_rows)
    x_ref = refs[0]
    shards = refs[1 : 1 + count]
    x_out = refs[1 + count]
    wholes = refs[2 + count : 2 + 2 * count]
    own_sem, x_send, x_recv = refs[2 + 2 * count : 5 + 2 * count]
    my_row = lax.axis_index("row")
    half_way = n_col // 2
    greet(n_col, n_row)
    hop, own_copy = ring_hops(by_rows, n_col, shards, wholes, refs[5 + 2 * count :])
    width = x_ref.shape[1]
    x_place = x_out.at[:, pl.ds(pl.multiple_of(my_row * width, 128), width)]

    def x_copy(step):
        return pltpu.make_async_remote_copy(
            src_ref=x_ref,
            dst_ref=x_place,
            send_sem=x_send.at[step],
            recv_sem=x_recv.at[step],
            device_id={"row": (my_row + step) % n_row},
            device_id_type=pl.DeviceIdType.MESH,
        )

    own = [own_copy(i, own_sem.at[i]) for i in range(count)]
    own.append(pltpu.make_async_copy(x_ref, x_place, own_sem.at[count]))
    for index in range(count):
        hop(index, 0, True).start()
        hop(index, 0, False).start()
    for step in range(1, n_row):
        x_copy(step).start()
    for copy in own:
        copy.start()
    for step in range(half_way):
        for index in range(count):
            for to_right in (True, False):
                hop(index, step, to_right).wait_recv()
                if step + 1 < half_way:
                    hop(index, step + 1, to_right).start()
    for step in range(half_way):
        for index in range(count):
            for to_right in (True, False):
                hop(index, step, to_right).wait_send()
    for step in range(1, n_row):
        x_copy(step).wait()
    for copy in own:
        copy.wait()


def gather_all(layer_input, shards, by_rows):
    n_col, n_row = lax.axis_size("col"), lax.axis_size("row")
    count = len(shards)
    half_way = n_col // 2
    shapes = [
        jax.ShapeDtypeStruct((layer_input.shape[0], layer_input.shape[1] * n_row), jnp.bfloat16)
    ] + [
        jax.ShapeDtypeStruct(whole_shape(shard, rows, n_col), jnp.bfloat16)
        for shard, rows in zip(shards, by_rows)
    ]
    return pl.pallas_call(
        functools.partial(gather_kernel, by_rows, n_col, n_row),
        out_shape=shapes,
        in_specs=[pl.BlockSpec(memory_space=pl.ANY)] * (1 + count),
        out_specs=[pl.BlockSpec(memory_space=pl.ANY)] * (1 + count),
        scratch_shapes=[
            pltpu.SemaphoreType.DMA((count + 1,)),
            pltpu.SemaphoreType.DMA((n_row,)),
            pltpu.SemaphoreType.DMA((n_row,)),
        ]
        + [pltpu.SemaphoreType.DMA((count, half_way))] * 4,
        compiler_params=pltpu.CompilerParams(collective_id=0, has_side_effects=True),
        name="gather_all",
    )(layer_input, *shards)


NT = (((1,), (1,)), ((), ()))


def columns_of(ref, index, width):
    if len(ref.shape) == 3:
        each = width // ref.shape[2]
        return jnp.concatenate([ref[index * each + i] for i in range(each)], axis=1)
    return ref[:, index * width : (index + 1) * width]


def layer_kernel(dims, *refs):
    n_col, n_row, heads, dec_count, page_count, score_scale = dims
    (
        bias_ref,
        q_ref,
        k_ref,
        v_ref,
        var_col,
        var_row,
        keep_row,
        ask_ref,
        facts_ref,
        slot_bias,
        page_var,
        pool_ref,
        pick_ref,
        own_ref,
        x_ref,
        norm_ref,
        wo_ref,
        wg_shard,
        wu_shard,
        wd_shard,
        tail_ref,
        hidden_ref,
        tail_out,
        wg_ref,
        wu_ref,
        wd_ref,
        asked,
        answer,
        answered,
        attended,
        part_send,
        part_recv,
        resid_all,
        normed,
        units,
        resid,
        own_sem,
        ask_send,
        ask_recv,
        ans_send,
        ans_recv,
        t_send,
        t_recv,
        row_send,
        row_recv,
        r_send,
        r_recv,
        l_send,
        l_recv,
    ) = refs
    me, my_row = lax.axis_index("col"), lax.axis_index("row")
    half_way = n_col // 2
    rows, width = x_ref.shape
    pre_len = rows - dec_count
    greet(n_col, n_row)
    hop, own_copy = ring_hops(
        (True, True, False),
        n_col,
        (wg_shard, wu_shard, wd_shard),
        (wg_ref, wu_ref, wd_ref),
        (r_send, r_recv, l_send, l_recv),
    )

    def to_peer(src, dst, send, recv, step):
        return pltpu.make_async_remote_copy(
            src_ref=src,
            dst_ref=dst,
            send_sem=send.at[step],
            recv_sem=recv.at[step],
            device_id={"col": (me + step) % n_col},
            device_id_type=pl.DeviceIdType.MESH,
        )

    def ask(step):
        return to_peer(
            ask_ref.at[(me + step) % n_col], asked.at[me], ask_send, ask_recv, step
        )

    def reply(step):
        return to_peer(
            answer.at[(me + step) % n_col], answered.at[me], ans_send, ans_recv, step
        )

    def tail(step):
        return to_peer(tail_ref.at[(me + step) % n_col], tail_out.at[me], t_send, t_recv, step)

    def to_row(src, dst, stage, step):
        return pltpu.make_async_remote_copy(
            src_ref=src,
            dst_ref=dst,
            send_sem=row_send.at[stage, step],
            recv_sem=row_recv.at[stage, step],
            device_id={"row": (my_row + step) % n_row},
            device_id_type=pl.DeviceIdType.MESH,
        )

    def scatter(stage, step):
        return to_row(
            part_send.at[stage, (my_row + step) % n_row],
            part_recv.at[stage, my_row],
            stage,
            step,
        )

    def spread(step):
        return to_row(resid_all.at[my_row], resid_all.at[my_row], 2, step)

    def pump(step):
        for index in range(3):
            for to_right in (True, False):
                hop(index, step, to_right).wait_recv()
                if step + 1 < half_way:
                    hop(index, step + 1, to_right).start()

    own_ask = pltpu.make_async_copy(ask_ref.at[me], asked.at[me], own_sem.at[3])
    own_tail = pltpu.make_async_copy(tail_ref.at[me], tail_out.at[me], own_sem.at[4])
    for step in range(1, n_col):
        ask(step).start()
    own_ask.start()
    for index in range(3):
        hop(index, 0, True).start()
        hop(index, 0, False).start()
    for index in range(3):
        own_copy(index, own_sem.at[index]).start()
    own_tail.start()

    block = 128
    lane_head = lax.broadcasted_iota(jnp.int32, (block, width), 1) // HD

    @pl.loop(0, pre_len // block)
    def _(at):
        start = pl.multiple_of(at * block, block)
        queries = q_ref[pl.ds(start, block), :]
        same = var_col[pl.ds(start, block), :] == var_row[...]
        query_at = lax.broadcasted_iota(jnp.int32, (block, pre_len), 0) + start
        key_at = lax.broadcasted_iota(jnp.int32, (block, pre_len), 1)
        allowed = (keep_row[...] == 1) | (query_at == key_at)
        result = jnp.zeros((block, width), jnp.float32)
        for head in range(heads):
            one = jnp.where(lane_head == head, queries.astype(jnp.float32), 0.0)
            scores = lax.dot_general(
                one.astype(jnp.bfloat16),
                k_ref[0:pre_len, :],
                NT,
                preferred_element_type=jnp.float32,
            )
            scores = scores * score_scale + jnp.where(same, bias_ref[0, head], bias_ref[1, head])
            weights = jnp.where(allowed, jnp.exp(scores), 0.0)
            weights = weights / jnp.sum(weights, axis=1, keepdims=True)
            mixed = jnp.dot(
                weights.astype(jnp.bfloat16),
                v_ref[0:pre_len, :],
                preferred_element_type=jnp.float32,
            )
            result = jnp.where(lane_head == head, mixed, result)
        attended[pl.ds(start, block), :] = result.astype(jnp.bfloat16)

    own_ask.wait()
    for step in range(1, n_col):
        ask(step).wait_recv()
    slots, page_size = asked.shape[0] * asked.shape[1], pool_ref.shape[2]
    queries = asked[...].reshape(slots, width).astype(jnp.bfloat16)
    facts = facts_ref[...]
    length = facts[:, page_count : page_count + 1]
    variate = facts[:, page_count + 1 : page_count + 2]
    same_bias, diff_bias = slot_bias[:, 0:1], slot_bias[:, 1:2]
    row_at = lax.broadcasted_iota(jnp.int32, (slots, page_size), 1)

    def one_page(page, carry):
        acc, total = carry
        scores = lax.dot_general(
            queries, pool_ref[page, 0], NT, preferred_element_type=jnp.float32
        )
        same = page_var[pl.ds(page, 1), :] == variate
        scores = scores * score_scale + jnp.where(same, same_bias, diff_bias)
        used = jnp.zeros((slots, page_size), jnp.float32)
        for entry in range(page_count):
            left_over = jnp.where(
                facts[:, entry : entry + 1] == page, length - entry * page_size, 0
            )
            used = used + jnp.where(row_at < left_over, 1.0, 0.0)
        weights = jnp.where(used > 0.0, used * jnp.exp(scores), 0.0)
        total = total + jnp.sum(weights, axis=1, keepdims=True)
        acc = acc + jnp.dot(
            weights.astype(jnp.bfloat16), pool_ref[page, 1], preferred_element_type=jnp.float32
        )
        return acc, total

    acc, total = lax.fori_loop(
        0,
        pool_ref.shape[0],
        one_page,
        (jnp.zeros((slots, width), jnp.float32), jnp.zeros((slots, 1), jnp.float32)),
    )
    mean = jnp.where(total > 0.0, acc / jnp.where(total > 0.0, total, 1.0), 0.0)
    answer[:, :, 0:width] = mean.reshape(n_col, slots // n_col, width)
    answer[:, :, width:] = jnp.broadcast_to(total, (slots, 128)).reshape(
        n_col, slots // n_col, 128
    )
    own_reply = pltpu.make_async_copy(answer.at[me], answered.at[me], own_sem.at[5])
    own_reply.start()
    for step in range(1, n_col):
        reply(step).start()
    pump(0)
    own_reply.wait()
    for step in range(1, n_col):
        reply(step).wait_recv()
    back = answered[...].reshape(slots, width + 128)
    slot_head = (lax.broadcasted_iota(jnp.int32, (slots, width), 0) % (slots // n_col)) % heads
    mine = lax.broadcasted_iota(jnp.int32, (slots, width), 1) // HD == slot_head
    pick = pick_ref[...]
    cached = jnp.dot(
        pick,
        jnp.where(mine, back[:, 0:width], 0.0),
        preferred_element_type=jnp.float32,
        precision=lax.Precision.HIGHEST,
    )
    cached_total = jnp.dot(
        pick,
        jnp.where(mine, jnp.broadcast_to(back[:, width : width + 1], (slots, width)), 0.0),
        preferred_element_type=jnp.float32,
        precision=lax.Precision.HIGHEST,
    )
    own_exp = own_ref[...]
    whole_total = cached_total + own_exp
    attended[pl.ds(pre_len, dec_count), :] = (
        cached * (cached_total / whole_total)
        + v_ref[pre_len:rows, :].astype(jnp.float32) * (own_exp / whole_total)
    ).astype(jnp.bfloat16)

    for target in range(n_row):
        part_send[0, target] = jnp.dot(
            attended[...], columns_of(wo_ref, target, width), preferred_element_type=jnp.float32
        ).astype(jnp.bfloat16)
    for step in range(1, n_row):
        scatter(0, step).start()
    pump(1)
    total_share = part_send[0, my_row].astype(jnp.float32) + x_ref[...].astype(jnp.float32)
    for step in range(1, n_row):
        scatter(0, step).wait_recv()
    for step in range(1, n_row):
        total_share = total_share + part_recv[0, (my_row + step) % n_row].astype(jnp.float32)
    resid[...] = total_share
    resid_all[my_row] = total_share.astype(jnp.bfloat16)
    for step in range(1, n_row):
        spread(step).start()
    for step in range(2, half_way):
        pump(step)
    for step in range(1, n_col):
        tail(step).start()
    for step in range(1, n_row):
        spread(step).wait_recv()
    squares = jnp.zeros((rows, 1), jnp.float32)
    for piece in range(n_row):
        values = resid_all[piece].astype(jnp.float32)
        squares = squares + jnp.sum(values * values, axis=1, keepdims=True)
    scale = lax.rsqrt(squares * (1.0 / (n_row * width)) + eps)
    for piece in range(n_row):
        cols = slice(piece * width, (piece + 1) * width)
        normed[:, cols] = (
            resid_all[piece].astype(jnp.float32) * scale * norm_ref[:, cols]
        ).astype(jnp.bfloat16)
    for index in range(3):
        own_copy(index, own_sem.at[index]).wait()

    tile = 256

    @pl.loop(0, units.shape[1] // tile)
    def _(at):
        cols = pl.ds(pl.multiple_of(at * tile, tile), tile)
        gate = jnp.dot(normed[...], wg_ref[:, cols], preferred_element_type=jnp.float32)
        up = jnp.dot(normed[...], wu_ref[:, cols], preferred_element_type=jnp.float32)
        units[:, cols] = (gate / (1.0 + jnp.exp(-gate)) * up).astype(jnp.bfloat16)

    for target in range(n_row):
        part_send[1, target] = jnp.dot(
            units[...], columns_of(wd_ref, target, width), preferred_element_type=jnp.float32
        ).astype(jnp.bfloat16)
    for step in range(1, n_row):
        scatter(1, step).start()
    total_share = resid[...] + part_send[1, my_row].astype(jnp.float32)
    for step in range(1, n_row):
        scatter(1, step).wait_recv()
    for step in range(1, n_row):
        total_share = total_share + part_recv[1, (my_row + step) % n_row].astype(jnp.float32)
    hidden_ref[...] = total_share.astype(jnp.bfloat16)

    for step in range(1, n_row):
        scatter(0, step).wait_send()
        scatter(1, step).wait_send()
        spread(step).wait_send()
    for step in range(1, n_col):
        ask(step).wait_send()
        reply(step).wait_send()
    for step in range(half_way):
        for index in range(3):
            for to_right in (True, False):
                hop(index, step, to_right).wait_send()
    own_tail.wait()
    for step in range(1, n_col):
        tail(step).wait()


def rest_of_layer(dims, *operands):
    n_col, n_row = dims[:2]
    x, wg, wu, wd, tails = operands[14], operands[17], operands[18], operands[19], operands[20]
    ask = operands[7]
    rows, width = x.shape
    half_way = n_col // 2
    full = n_row * width
    vmem = pl.BlockSpec(memory_space=pltpu.VMEM)
    anywhere = pl.BlockSpec(memory_space=pl.ANY)
    dma = pltpu.SemaphoreType.DMA
    return pl.pallas_call(
        functools.partial(layer_kernel, dims),
        out_shape=[
            jax.ShapeDtypeStruct((rows, width), jnp.bfloat16),
            jax.ShapeDtypeStruct(tails.shape, jnp.bfloat16),
        ],
        in_specs=[pl.BlockSpec(memory_space=pltpu.SMEM)] + [vmem] * 19 + [anywhere],
        out_specs=[vmem, anywhere],
        scratch_shapes=[
            pltpu.VMEM(whole_shape(wg, True, n_col), jnp.bfloat16),
            pltpu.VMEM(whole_shape(wu, True, n_col), jnp.bfloat16),
            pltpu.VMEM(whole_shape(wd, False, n_col), jnp.bfloat16),
            pltpu.VMEM(ask.shape, jnp.float32),
            pltpu.VMEM(ask.shape[:2] + (width + 128,), jnp.float32),
            pltpu.VMEM(ask.shape[:2] + (width + 128,), jnp.float32),
            pltpu.VMEM((rows, width), jnp.bfloat16),
            pltpu.VMEM((2, n_row, rows, width), jnp.bfloat16),
            pltpu.VMEM((2, n_row, rows, width), jnp.bfloat16),
            pltpu.VMEM((n_row, rows, width), jnp.bfloat16),
            pltpu.VMEM((rows, full), jnp.bfloat16),
            pltpu.VMEM((rows, wg.shape[1]), jnp.bfloat16),
            pltpu.VMEM((rows, width), jnp.float32),
            dma((6,)),
        ]
        + [dma((n_col,))] * 6
        + [dma((3, n_row))] * 2
        + [dma((3, half_way))] * 4,
        compiler_params=pltpu.CompilerParams(
            collective_id=1, has_side_effects=True, vmem_limit_bytes=50 * 1024 * 1024
        ),
        name="rest_of_layer",
    )(*operands)


def on_device(
    layer_input,
    w_q,
    w_k,
    w_v,
    w_o,
    w_gate,
    w_up,
    w_down,
    norm1,
    norm2,
    q_gain,
    k_gain,
    bias_same,
    bias_diff,
    pre_variate,
    pre_keep,
    dec_variate,
    dec_len,
    dec_table,
    dec_holder,
    kv_pool,
    page_variates,
):
    row_count = layer_input.shape[0]
    local_width = layer_input.shape[1]
    pre_len = pre_variate.shape[1]
    dec_count = dec_len.shape[0]
    heads_here = local_width // HD
    score_scale = HD ** (-0.5)
    page_size = kv_pool.shape[2]
    page_count = dec_table.shape[1]
    peer_count = lax.axis_size("col")
    slot_count = max(2, (dec_count + peer_count - 1) // peer_count)
    holder = dec_holder[:, 0]
    onehot = (holder[:, None] == jnp.arange(peer_count)[None, :]).astype(jnp.int32)
    slot_rank = jnp.sum((jnp.cumsum(onehot, axis=0) - onehot) * onehot, axis=1)
    target = holder * slot_count + slot_rank
    int_facts = jnp.concatenate([dec_table, dec_len[:, None], dec_variate[:, None]], axis=1)
    all_slots = peer_count * slot_count
    to_slot = target[None, :] == jnp.arange(all_slots)[:, None]
    send_int = jnp.sum(jnp.where(to_slot[:, :, None], int_facts[None], 0), axis=1)
    send_int = send_int.reshape(peer_count, slot_count, page_count + 2)
    int_part = lax.all_to_all(send_int, "col", split_axis=0, concat_axis=0, tiled=True)
    slot_ints = int_part.reshape(all_slots, page_count + 2)
    slot_table = slot_ints[:, :page_count]
    slot_len = slot_ints[:, page_count]
    slot_variate = slot_ints[:, page_count + 1]
    last_place = (slot_len // page_size)[:, None] == jnp.arange(page_count)[None, :]
    last_page = jnp.sum(jnp.where(last_place, slot_table, 0), axis=1)
    tail_send = kv_pool[last_page].reshape(peer_count, slot_count, 2, page_size, local_width)

    gathered_input, full_q, full_k, full_v, full_o = gather_all(
        layer_input, (w_q, w_k, w_v, w_o), (True, True, True, False)
    )
    normed = norm_rows(gathered_input.astype(jnp.float32), norm1).astype(jnp.bfloat16)
    queries = jnp.dot(normed, full_q, preferred_element_type=jnp.float32)
    keys_proj = jnp.dot(normed, full_k, preferred_element_type=jnp.float32)
    values_proj = jnp.dot(normed, full_v, preferred_element_type=jnp.float32)
    places = jnp.concatenate([segment_time(pre_variate[0]), dec_len])
    query_rot = rotate(
        norm_rows(queries.reshape(row_count, heads_here, HD), q_gain.reshape(heads_here, HD)),
        places,
    ).astype(jnp.bfloat16)
    key_rot = rotate(
        norm_rows(keys_proj.reshape(row_count, heads_here, HD), k_gain.reshape(heads_here, HD)),
        places,
    ).astype(jnp.bfloat16)
    value_bf = values_proj.astype(jnp.bfloat16).reshape(row_count, heads_here, HD)

    flat_query = query_rot.reshape(row_count, local_width)
    flat_key = key_rot.reshape(row_count, local_width)
    flat_value = value_bf.reshape(row_count, local_width)

    used_rows = slot_count * heads_here
    slot_rows = -(-used_rows // 8) * 8
    sent_query = jnp.dot(
        to_slot.astype(jnp.bfloat16), flat_query[pre_len:], preferred_element_type=jnp.float32
    )
    lane_head = jnp.arange(local_width) // HD
    head_rows = (jnp.arange(heads_here)[:, None] == lane_head[None, :]).astype(jnp.float32)
    ask = (sent_query[:, None, :] * head_rows[None]).reshape(peer_count, used_rows, local_width)
    ask = jnp.pad(ask, ((0, 0), (0, slot_rows - used_rows), (0, 0)))

    def per_row(values):
        wide = jnp.broadcast_to(
            values.reshape(peer_count, slot_count, 1, -1),
            (peer_count, slot_count, heads_here, values.shape[-1]),
        ).reshape(peer_count, used_rows, -1)
        wide = jnp.pad(wide, ((0, 0), (0, slot_rows - used_rows), (0, 0)))
        return wide.reshape(peer_count * slot_rows, -1)

    facts = per_row(slot_ints)
    bias_pair = jnp.stack([bias_same, bias_diff], axis=1)
    slot_bias = jnp.tile(
        jnp.pad(jnp.tile(bias_pair, (slot_count, 1)), ((0, slot_rows - used_rows), (0, 0))),
        (peer_count, 1),
    )
    pick = per_row(to_slot.astype(jnp.float32)).T
    own_score = (
        jnp.sum(
            query_rot[pre_len:].astype(jnp.float32) * key_rot[pre_len:].astype(jnp.float32), axis=2
        )
        * score_scale
        + bias_same[None]
    )
    own_exp = jnp.repeat(jnp.exp(own_score), HD, axis=1)
    hidden, tail_back = rest_of_layer(
        (peer_count, lax.axis_size("row"), heads_here, dec_count, page_count, score_scale),
        jnp.stack([bias_same, bias_diff]),
        flat_query,
        flat_key,
        flat_value,
        pre_variate[0][:, None],
        pre_variate,
        pre_keep,
        ask,
        facts,
        slot_bias,
        page_variates,
        kv_pool,
        pick,
        own_exp,
        layer_input,
        norm2[None],
        full_o,
        w_gate,
        w_up,
        w_down,
        tail_send,
    )
    old_tails = tail_back.reshape(all_slots, 2, page_size, local_width)[target]
    hit_row = (jnp.arange(page_size)[None, :] == (dec_len % page_size)[:, None])[:, None, :, None]
    new_rows = jnp.stack([flat_key[pre_len:], flat_value[pre_len:]], axis=1)[:, :, None, :]
    tail_pages = jnp.where(hit_row, new_rows, old_tails)
    prefill_pages = jnp.stack(
        [
            key_rot[:pre_len].reshape(pre_len // page_size, page_size, local_width),
            value_bf[:pre_len].reshape(pre_len // page_size, page_size, local_width),
        ],
        axis=1,
    )
    return (hidden, prefill_pages, tail_pages)


def solution(mesh):
    placed = (
        P("col", "row"),
        P("col", "row"),
        P("col", "row"),
        P("col", "row"),
        P("row", "col"),
        P("col", "row"),
        P("col", "row"),
        P("row", "col"),
        P(),
        P(),
        P("row"),
        P("row"),
        P("row"),
        P("row"),
        P("col", None),
        P("col", None),
        P("col"),
        P("col"),
        P("col", None),
        P("col", None),
        P("col", None, None, "row"),
        P("col", None),
    )
    return jax.shard_map(
        on_device,
        mesh=mesh,
        in_specs=placed,
        out_specs=(P("col", "row"), P("col", None, None, "row"), P("col", None, None, "row")),
        check_vma=False,
    )
```

time: 325 us -> 177 us (0.54)
  waiting for transfers between devices: 58.8 us -> 0.01 us
  local copies, waits for them, and re-layouts: 42.1 us -> 12.3 us
  matrix products: 32.2 us -> 3.53 us
  other arithmetic: 29.8 us -> 8.85 us
  Pallas kernels: 129 us -> 143 us
  between operations: 14.6 us -> 1.13 us
  starting transfers between devices: 15.9 us -> 5.72 us
    pallas_call x0 -> x1, Pallas kernels: none -> 118 us  [rest_of_layer(): pl.pallas_call(functools.partial(layer_kernel, dims), out_shape=[jax.Shap...]
    pallas_call x1, Pallas kernels: 129 us -> 25.4 us  [gather_all(): pl.pallas_call(functools.partial(gather_kernel, by_rows, n_col, n_row), o...]
    psum x1 -> x0, waiting for transfers between devices: 37.8 us -> none  [on_device(): lax.psum(partial_out.astype(jnp.bfloat16), 'row').astype(jnp.float32)]
    dot_general x9 -> x1, matrix products: 28.9 us -> 0.13 us  [on_device(): jnp.dot(to_slot.astype(jnp.bfloat16), flat_query[pre_len:], preferred_ele...]
    reduce_scatter x1 -> x0, waiting for transfers between devices: 20.9 us -> none  [on_device(): lax.psum_scatter(partial_ffn.astype(jnp.bfloat16), 'row', scatter_dimensi...]
    all_to_all x2 -> x0, starting transfers between devices: 9.96 us -> none  [the longest x1 5.44 us: on_device(): lax.all_to_all(attended.astype(jnp.bfloat16).reshape(peer_count, slot_cou...]
    broadcast_in_dim x8 -> x3, local copies, waits for them, and re-layouts: 8.85 us -> 0.09 us  [the longest x1 0.08 us: on_device(): own_exp = jnp.repeat(jnp.exp(own_score), HD, axis=1)]
    convert_element_type x7 -> x3, other arithmetic: 7.15 us -> 0.14 us  [the longest x1 0.07 us: on_device(): pick = per_row(to_slot.astype(jnp.float32)).T]
  transfers between devices with their start and end apart: 5 -> 1, of which waited for: 2 -> 0; matrix products, arithmetic and copies ran while one was open for 15% -> 6% of each run, Pallas kernels for 0% -> 15%
where the time goes in v2:
time: 177 us; the launch traced here: 175 us
  Pallas kernels  143 us (81%)
  local copies, waits for them, and re-layouts  12.3 us (7%)
  other arithmetic  8.85 us (5%)
  starting transfers between devices  5.72 us (3%)
  matrix products  3.53 us (2%)
    pallas_call x1, Pallas kernels, rest_of_layer(): pl.pallas_call(functools.partial(layer_kernel, dims), out_shape=[jax.Shap...  118 us
    pallas_call x1, Pallas kernels, gather_all(): pl.pallas_call(functools.partial(gather_kernel, by_rows, n_col, n_row), o...  25.4 us
    all_to_all x1, starting transfers between devices, on_device(): lax.all_to_all(send_int, 'col', split_axis=0, concat_axis=0, tiled=True)  5.72 us
    gather x1, local copies, waits for them, and re-layouts, on_device(): kv_pool[last_page]  4.29 us
  transfers between devices with their start and end apart: 1, of which 0 were waited for; matrix products, arithmetic and copies ran while one was open for 6% of the time, Pallas kernels for 15%

profile of v2, /device:TPU:9, one launch (start us, length us, event | category | flops | bytes accessed | tf_op | source)
XLA Modules:
  0.0 174.7 jit_solution(4237862292032679058)
XLA Ops:
  0.6 0.7 fusion.4
  1.4 0.8 select_reduce_fusion.1
  2.2 0.7 multiply_add_fusion.3
  2.9 0.7 pad_add_fusion
  3.6 0.2 select_reduce_fusion
  3.9 0.7 copy.128
  4.6 5.7 %all-to-all-start = ((s32[8,2,10]{2,1,0:T(2,128)}), s32[8,2,10]{2,1,0:T(2,128)S(1)}, u32[]{:S(2)}, u32[]{:S(2)}) async-start(s32[8,2,10]{2,1,0:T(2,128)} %bitcast.13), calls=%async_computation | async-start | bytes 16384 | tf_op jit(solution)/shard_map/all_to_all | solution.py:626
  10.3 0.8 mul.211
  11.1 25.4 %gather_all.1 = (bf16[528,1024]{1,0:T(8,128)(2,1)}, bf16[1024,256]{1,0:T(8,128)(2,1)}, bf16[1024,256]{1,0:T(8,128)(2,1)}, bf16[1024,256]{1,0:T(8,128)(2,1)}, bf16[256,1024]{1,0:T(8,128)(2,1)}) custom-call(bf16[528,256]{1,0:T(8,128)(2,1)} %refs_14_.1, bf16[128,256]{1,0:T(8,128)(2,1)} %refs_1_.1, bf16[128,256]{1,0:T(8,128)(2,1)} %refs_2_.1, ...), custom_call_target="tpu_custom_call" | custom-call | tf_op jit(solution)/shard_map/gather_all/pallas_call | solution.py:207
  36.6 1.7 fusion
  38.2 2.1 %multiply_reduce_fusion = (f32[528,4]{0,1:T(4,128)S(1)}, f32[528,256]{0,1:T(8,128)S(1)}) fusion(bf16[1024,256]{1,0:T(8,128)(2,1)} %get-tuple-element.12, bf16[528,1024]{1,0:T(8,128)(2,1)} %get-tuple-element.10, f32[1024]{0:T(1024)} %param.30, f32[528]{0:T(1024)S(1)} %add_rsqrt_fusion.2), kind=kOutput, calls=%fused_computation.12 | convolution fusion | flops 279254976 | bytes 2160960 | tf_op jit(solution)/shard_map/dot_general | solution.py:640
  40.5 0.3 reduce-window.9
  41.3 0.8 multiply_reduce_fusion.1
  42.1 0.4 multiply_cosine_fusion
  42.4 0.1 multiply_multiply_fusion
  42.7 0.2 multiply_subtract_fusion
  43.1 0.3 copy-done.11
  43.3 0.4 copy-done.15
  43.7 0.5 convolution_convert_fusion.refs_3_
  44.3 0.1 fusion.10
  44.7 0.2 copy.136
  45.2 0.4 pad_maximum_fusion
  45.6 0.2 copy.132.refs_1_
  45.8 0.2 copy.133.refs_2_
  45.9 0.1 copy.134.refs_4_
  46.4 1.1 copy.139
  47.8 0.2 fusion.3
  48.1 4.3 %gather_fusion = bf16[16,2,128,256]{3,2,1,0:T(8,128)(2,1)} fusion(bf16[32,2,128,256]{3,2,1,0:T(8,128)(2,1)} %refs_11_.1, s32[1024]{0:T(1024)S(1)} %pad_clamp_fusion.1), kind=kCustom, calls=%fused_computation | custom fusion | bytes 4194368 | tf_op jit(solution)/shard_map/gather | solution.py:633
  52.4 117.8 %rest_of_layer.1 = (bf16[528,256]{1,0:T(8,128)(2,1)S(1)}, bf16[8,2,2,128,256]{4,3,2,1,0:T(8,128)(2,1)}) custom-call(f32[2,4]{1,0:T(2,128)S(1)} %pad_maximum_fusion.2.refs_0_, bf16[528,256]{1,0:T(8,128)(2,1)S(1)} %copy.132.refs_1_, bf16[528,256]{1,0:T(8,128)(2,1)S(1)} %copy.133.refs_2_, bf16[528,256]{1,0:T(8,128)(2,1)S(1)} %convolution_convert_fusion.refs_3_, ...), custom_call_target="tpu_custom_call" | custom-call | tf_op jit(solution)/shard_map/rest_of_layer/pallas_call | solution.py:549
  170.2 2.3 %gather_fusion.1 = bf16[16,2,128,256]{3,2,1,0:T(8,128)(2,1)S(1)} fusion(bf16[16,2,128,256]{3,2,1,0:T(8,128)(2,1)} %bitcast.63, s32[1024]{0:T(1024)S(1)} %pad_clamp_fusion), kind=kCustom, calls=%fused_computation.1 | custom fusion | bytes 4194368 | tf_op jit(solution)/shard_map/gather | solution.py:714
  172.5 1.5 broadcast_select_fusion
  174.0 0.7 copy.149
  (88 shorter events, 2.1 us)
Async XLA Ops:
  4.6 43.0 %all-to-all-start = ((s32[8,2,10]{2,1,0:T(2,128)}), s32[8,2,10]{2,1,0:T(2,128)S(1)}, u32[]{:S(2)}, u32[]{:S(2)}) async-start(s32[8,2,10]{2,1,0:T(2,128)} %bitcast.13), calls=%async_computation | async-start | bytes 16384 | tf_op jit(solution)/shard_map/all_to_all | solution.py:626
  36.5 3.9 %copy-start.5 = (s32[1,512]{1,0:T(1,128)S(1)}, s32[1,512]{1,0:T(1,128)}, u32[]{:S(2)}) copy-start(s32[1,512]{1,0:T(1,128)} %refs_5_.1) | copy-start | bytes 6148
  36.5 4.7 %copy-start.13 = (s32[16]{0:T(128)S(1)}, s32[16]{0:T(128)}, u32[]{:S(2)}) copy-start(s32[16]{0:T(128)} %param.39) | copy-start | bytes 196
  36.5 4.7 %copy-start.14 = (f32[256]{0:T(256)S(1)}, f32[256]{0:T(256)}, u32[]{:S(2)}) copy-start(f32[256]{0:T(256)} %param.32) | copy-start | bytes 3076
  36.5 4.7 %copy-start.9 = (bf16[528,1024]{1,0:T(8,128)(2,1)S(1)}, bf16[528,1024]{1,0:T(8,128)(2,1)}, u32[]{:S(2)}) copy-start(bf16[528,1024]{1,0:T(8,128)(2,1)} %get-tuple-element.10) | copy-start | bytes 3244036
  36.5 4.7 %copy-start.16 = (bf16[1024,256]{1,0:T(8,128)(2,1)S(1)}, bf16[1024,256]{1,0:T(8,128)(2,1)}, u32[]{:S(2)}) copy-start(bf16[1024,256]{1,0:T(8,128)(2,1)} %get-tuple-element.11) | copy-start | bytes 1572868
  36.5 4.7 %copy-start.17 = (f32[1024]{0:T(1024)S(1)}, f32[1024]{0:T(1024)}, u32[]{:S(2)}) copy-start(f32[1024]{0:T(1024)} %param.30) | copy-start | bytes 12292
  42.7 0.7 copy-start.11
  42.7 1.0 copy-start.15
  43.0 1.4 copy-start.10
  43.0 1.4 copy-start.12
  48.0 4.4 %copy-start = (bf16[528,256]{1,0:T(8,128)(2,1)S(1)}, bf16[528,256]{1,0:T(8,128)(2,1)}, u32[]{:S(2)}) copy-start(bf16[528,256]{1,0:T(8,128)(2,1)} %refs_14_.1) | copy-start | bytes 811012
  48.0 4.4 %copy-start.1 = (bf16[256,1024]{1,0:T(8,128)(2,1)S(1)}, bf16[256,1024]{1,0:T(8,128)(2,1)}, u32[]{:S(2)}) copy-start(bf16[256,1024]{1,0:T(8,128)(2,1)} %get-tuple-element.14.refs_16_) | copy-start | bytes 1572868
  48.0 4.4 %copy-start.2 = (bf16[128,1024]{1,0:T(8,128)(2,1)S(1)}, bf16[128,1024]{1,0:T(8,128)(2,1)}, u32[]{:S(2)}) copy-start(bf16[128,1024]{1,0:T(8,128)(2,1)} %refs_17_.1) | copy-start | bytes 786436
  48.0 4.4 %copy-start.3 = (bf16[128,1024]{1,0:T(8,128)(2,1)S(1)}, bf16[128,1024]{1,0:T(8,128)(2,1)}, u32[]{:S(2)}) copy-start(bf16[128,1024]{1,0:T(8,128)(2,1)} %refs_18_.1) | copy-start | bytes 786436
  48.0 4.4 %copy-start.4 = (bf16[1024,128]{1,0:T(8,128)(2,1)S(1)}, bf16[1024,128]{1,0:T(8,128)(2,1)}, u32[]{:S(2)}) copy-start(bf16[1024,128]{1,0:T(8,128)(2,1)} %refs_19_.1) | copy-start | bytes 786436
  48.0 4.4 %copy-start.6 = (s32[32,128]{1,0:T(8,128)S(1)}, s32[32,128]{1,0:T(8,128)}, u32[]{:S(2)}) copy-start(s32[32,128]{1,0:T(8,128)} %refs_10_.1) | copy-start | bytes 49156
  48.0 4.4 %copy-start.7 = (f32[1024]{0:T(1024)S(1)}, f32[1024]{0:T(1024)}, u32[]{:S(2)}) copy-start(f32[1024]{0:T(1024)} %param.31) | copy-start | bytes 12292
  48.0 4.4 %copy-start.8 = (s32[1,512]{1,0:T(1,128)S(1)}, s32[1,512]{1,0:T(1,128)}, u32[]{:S(2)}) copy-start(s32[1,512]{1,0:T(1,128)} %refs_6_.1) | copy-start | bytes 6148

commit v3 on v2

--- a/solution.py
+++ b/solution.py
@@ -216,6 +216,9 @@
         ]
         + [pltpu.SemaphoreType.DMA((count, half_way))] * 4,
         compiler_params=pltpu.CompilerParams(collective_id=0, has_side_effects=True),
+        cost_estimate=pl.CostEstimate(
+            flops=0, bytes_accessed=80_000_000, transcendentals=0
+        ),
         name="gather_all",
     )(layer_input, *shards)
 
@@ -227,11 +230,11 @@
     if len(ref.shape) == 3:
         each = width // ref.shape[2]
         return jnp.concatenate([ref[index * each + i] for i in range(each)], axis=1)
-    return ref[:, index * width : (index + 1) * width]
+    return ref[:, pl.ds(pl.multiple_of(index * width, 128), width)]
 
 
 def layer_kernel(dims, *refs):
-    n_col, n_row, heads, dec_count, page_count, score_scale = dims
+    n_col, n_row, heads, dec_count, page_count, score_scale, tail_shifts = dims
     (
         bias_ref,
         q_ref,
@@ -263,8 +266,10 @@
         answer,
         answered,
         attended,
-        part_send,
-        part_recv,
+        pair_send,
+        pair_recv,
+        sum_send,
+        sum_recv,
         resid_all,
         normed,
         units,
@@ -276,8 +281,14 @@
         ans_recv,
         t_send,
         t_recv,
-        row_send,
-        row_recv,
+        pair_send_sem,
+        pair_recv_sem,
+        sum_send_sem,
+        sum_recv_sem,
+        far_send_sem,
+        far_recv_sem,
+        near_send_sem,
+        near_recv_sem,
         r_send,
         r_recv,
         l_send,
@@ -316,29 +327,98 @@
             answer.at[(me + step) % n_col], answered.at[me], ans_send, ans_recv, step
         )
 
-    def tail(step):
-        return to_peer(tail_ref.at[(me + step) % n_col], tail_out.at[me], t_send, t_recv, step)
-
-    def to_row(src, dst, stage, step):
+    def tail(at):
+        return pltpu.make_async_remote_copy(
+            src_ref=tail_ref.at[at],
+            dst_ref=tail_out.at[at],
+            send_sem=t_send.at[at],
+            recv_sem=t_recv.at[at],
+            device_id={"col": (me + tail_shifts[at]) % n_col},
+            device_id_type=pl.DeviceIdType.MESH,
+        )
+
+    chips = n_row // 2
+    chip, core = my_row // 2, my_row % 2
+
+    def to_row(src, dst, send, recv, target):
         return pltpu.make_async_remote_copy(
             src_ref=src,
             dst_ref=dst,
-            send_sem=row_send.at[stage, step],
-            recv_sem=row_recv.at[stage, step],
-            device_id={"row": (my_row + step) % n_row},
+            send_sem=send,
+            recv_sem=recv,
+            device_id={"row": target},
             device_id_type=pl.DeviceIdType.MESH,
         )
 
-    def scatter(stage, step):
+    def chip_at(step):
+        return (chip + step) % chips
+
+    def pair(stage, step):
+        there = chip_at(step)
         return to_row(
-            part_send.at[stage, (my_row + step) % n_row],
-            part_recv.at[stage, my_row],
-            stage,
-            step,
-        )
-
-    def spread(step):
-        return to_row(resid_all.at[my_row], resid_all.at[my_row], 2, step)
+            pair_send.at[stage, there],
+            pair_recv.at[stage, there],
+            pair_send_sem.at[stage, step],
+            pair_recv_sem.at[stage, step],
+            chip * 2 + 1 - core,
+        )
+
+    def summed(stage, step):
+        there = chip_at(step)
+        return to_row(
+            sum_send.at[stage, there],
+            sum_recv.at[stage, chip],
+            sum_send_sem.at[stage, step],
+            sum_recv_sem.at[stage, step],
+            there * 2 + core,
+        )
+
+    def far(step):
+        return to_row(
+            resid_all.at[my_row],
+            resid_all.at[my_row],
+            far_send_sem.at[step],
+            far_recv_sem.at[step],
+            chip_at(step) * 2 + core,
+        )
+
+    def near(step):
+        held = ((chip + chips - step) % chips) * 2 + core
+        return to_row(
+            resid_all.at[held],
+            resid_all.at[held],
+            near_send_sem.at[step],
+            near_recv_sem.at[step],
+            chip * 2 + 1 - core,
+        )
+
+    def reduce_start(stage, left, weight):
+        def product(target):
+            return jnp.dot(
+                left[...], columns_of(weight, target, width), preferred_element_type=jnp.float32
+            )
+
+        steps = tuple(range(1, chips)) + (0,)
+        for step in steps:
+            there = chip_at(step)
+            pair_send[stage, there] = product(there * 2 + 1 - core).astype(jnp.bfloat16)
+            pair(stage, step).start()
+        for step in steps:
+            there = chip_at(step)
+            mine = product(there * 2 + core)
+            pair(stage, step).wait_recv()
+            mine = mine + pair_recv[stage, there].astype(jnp.float32)
+            if step == 0:
+                return mine
+            sum_send[stage, there] = mine.astype(jnp.bfloat16)
+            summed(stage, step).start()
+
+    def reduce_end(stage, total_share):
+        for step in range(1, chips):
+            summed(stage, step).wait_recv()
+            there = (chip + chips - step) % chips
+            total_share = total_share + sum_recv[stage, there].astype(jnp.float32)
+        return total_share
 
     def pump(step):
         for index in range(3):
@@ -348,7 +428,6 @@
                     hop(index, step + 1, to_right).start()
 
     own_ask = pltpu.make_async_copy(ask_ref.at[me], asked.at[me], own_sem.at[3])
-    own_tail = pltpu.make_async_copy(tail_ref.at[me], tail_out.at[me], own_sem.at[4])
     for step in range(1, n_col):
         ask(step).start()
     own_ask.start()
@@ -357,7 +436,6 @@
         hop(index, 0, False).start()
     for index in range(3):
         own_copy(index, own_sem.at[index]).start()
-    own_tail.start()
 
     block = 128
     lane_head = lax.broadcasted_iota(jnp.int32, (block, width), 1) // HD
@@ -463,28 +541,23 @@
         + v_ref[pre_len:rows, :].astype(jnp.float32) * (own_exp / whole_total)
     ).astype(jnp.bfloat16)
 
-    for target in range(n_row):
-        part_send[0, target] = jnp.dot(
-            attended[...], columns_of(wo_ref, target, width), preferred_element_type=jnp.float32
-        ).astype(jnp.bfloat16)
-    for step in range(1, n_row):
-        scatter(0, step).start()
+    resid[...] = reduce_start(0, attended, wo_ref) + x_ref[...].astype(jnp.float32)
     pump(1)
-    total_share = part_send[0, my_row].astype(jnp.float32) + x_ref[...].astype(jnp.float32)
-    for step in range(1, n_row):
-        scatter(0, step).wait_recv()
-    for step in range(1, n_row):
-        total_share = total_share + part_recv[0, (my_row + step) % n_row].astype(jnp.float32)
+    total_share = reduce_end(0, resid[...])
     resid[...] = total_share
     resid_all[my_row] = total_share.astype(jnp.bfloat16)
-    for step in range(1, n_row):
-        spread(step).start()
+    for step in range(1, chips):
+        far(step).start()
+    near(0).start()
     for step in range(2, half_way):
         pump(step)
-    for step in range(1, n_col):
-        tail(step).start()
-    for step in range(1, n_row):
-        spread(step).wait_recv()
+    for at in range(len(tail_shifts)):
+        tail(at).start()
+    for step in range(1, chips):
+        far(step).wait_recv()
+        near(step).start()
+    for step in range(chips):
+        near(step).wait_recv()
     squares = jnp.zeros((rows, 1), jnp.float32)
     for piece in range(n_row):
         values = resid_all[piece].astype(jnp.float32)
@@ -507,23 +580,19 @@
         up = jnp.dot(normed[...], wu_ref[:, cols], preferred_element_type=jnp.float32)
         units[:, cols] = (gate / (1.0 + jnp.exp(-gate)) * up).astype(jnp.bfloat16)
 
-    for target in range(n_row):
-        part_send[1, target] = jnp.dot(
-            units[...], columns_of(wd_ref, target, width), preferred_element_type=jnp.float32
-        ).astype(jnp.bfloat16)
-    for step in range(1, n_row):
-        scatter(1, step).start()
-    total_share = resid[...] + part_send[1, my_row].astype(jnp.float32)
-    for step in range(1, n_row):
-        scatter(1, step).wait_recv()
-    for step in range(1, n_row):
-        total_share = total_share + part_recv[1, (my_row + step) % n_row].astype(jnp.float32)
-    hidden_ref[...] = total_share.astype(jnp.bfloat16)
-
-    for step in range(1, n_row):
-        scatter(0, step).wait_send()
-        scatter(1, step).wait_send()
-        spread(step).wait_send()
+    resid[...] = reduce_start(1, units, wd_ref) + resid[...]
+    hidden_ref[...] = reduce_end(1, resid[...]).astype(jnp.bfloat16)
+
+    for at in range(len(tail_shifts)):
+        tail(at).wait()
+    for step in range(chips):
+        pair(0, step).wait_send()
+        pair(1, step).wait_send()
+        near(step).wait_send()
+    for step in range(1, chips):
+        summed(0, step).wait_send()
+        summed(1, step).wait_send()
+        far(step).wait_send()
     for step in range(1, n_col):
         ask(step).wait_send()
         reply(step).wait_send()
@@ -531,9 +600,6 @@
         for index in range(3):
             for to_right in (True, False):
                 hop(index, step, to_right).wait_send()
-    own_tail.wait()
-    for step in range(1, n_col):
-        tail(step).wait()
 
 
 def rest_of_layer(dims, *operands):
@@ -542,6 +608,7 @@
     ask = operands[7]
     rows, width = x.shape
     half_way = n_col // 2
+    chips = n_row // 2
     full = n_row * width
     vmem = pl.BlockSpec(memory_space=pltpu.VMEM)
     anywhere = pl.BlockSpec(memory_space=pl.ANY)
@@ -562,19 +629,26 @@
             pltpu.VMEM(ask.shape[:2] + (width + 128,), jnp.float32),
             pltpu.VMEM(ask.shape[:2] + (width + 128,), jnp.float32),
             pltpu.VMEM((rows, width), jnp.bfloat16),
-            pltpu.VMEM((2, n_row, rows, width), jnp.bfloat16),
-            pltpu.VMEM((2, n_row, rows, width), jnp.bfloat16),
+            pltpu.VMEM((2, chips, rows, width), jnp.bfloat16),
+            pltpu.VMEM((2, chips, rows, width), jnp.bfloat16),
+            pltpu.VMEM((2, chips, rows, width), jnp.bfloat16),
+            pltpu.VMEM((2, chips, rows, width), jnp.bfloat16),
             pltpu.VMEM((n_row, rows, width), jnp.bfloat16),
             pltpu.VMEM((rows, full), jnp.bfloat16),
             pltpu.VMEM((rows, wg.shape[1]), jnp.bfloat16),
             pltpu.VMEM((rows, width), jnp.float32),
             dma((6,)),
         ]
-        + [dma((n_col,))] * 6
-        + [dma((3, n_row))] * 2
+        + [dma((n_col,))] * 4
+        + [dma((tails.shape[0],))] * 2
+        + [dma((2, chips))] * 4
+        + [dma((chips,))] * 4
         + [dma((3, half_way))] * 4,
         compiler_params=pltpu.CompilerParams(
             collective_id=1, has_side_effects=True, vmem_limit_bytes=50 * 1024 * 1024
+        ),
+        cost_estimate=pl.CostEstimate(
+            flops=200_000_000_000, bytes_accessed=200_000_000, transcendentals=2_000_000
         ),
         name="rest_of_layer",
     )(*operands)
@@ -630,8 +704,21 @@
     slot_variate = slot_ints[:, page_count + 1]
     last_place = (slot_len // page_size)[:, None] == jnp.arange(page_count)[None, :]
     last_page = jnp.sum(jnp.where(last_place, slot_table, 0), axis=1)
-    tail_send = kv_pool[last_page].reshape(peer_count, slot_count, 2, page_size, local_width)
-
+    my_col = lax.axis_index("col")
+    shift_peer = (my_col + jnp.arange(peer_count)) % peer_count
+    tail_send = kv_pool[last_page.reshape(peer_count, slot_count)[shift_peer].reshape(-1)]
+    tail_send = tail_send.reshape(peer_count, slot_count, 2, page_size, local_width)
+    first_shift = max(peer_count // 2 - 2, 1)
+    last_shift = min(first_shift + 5, peer_count)
+    kernel_shifts = tuple(range(1, first_shift)) + tuple(range(last_shift, peer_count))
+    tail_parts = {0: tail_send[0]}
+    for shift in range(first_shift, last_shift):
+        tail_parts[shift] = lax.ppermute(
+            tail_send[shift],
+            "col",
+            [(source, (source + shift) % peer_count) for source in range(peer_count)],
+        )
+    kernel_tails = jnp.stack([tail_send[shift] for shift in kernel_shifts])
     gathered_input, full_q, full_k, full_v, full_o = gather_all(
         layer_input, (w_q, w_k, w_v, w_o), (True, True, True, False)
     )
@@ -688,7 +775,15 @@
     )
     own_exp = jnp.repeat(jnp.exp(own_score), HD, axis=1)
     hidden, tail_back = rest_of_layer(
-        (peer_count, lax.axis_size("row"), heads_here, dec_count, page_count, score_scale),
+        (
+            peer_count,
+            lax.axis_size("row"),
+            heads_here,
+            dec_count,
+            page_count,
+            score_scale,
+            kernel_shifts,
+        ),
         jnp.stack([bias_same, bias_diff]),
         flat_query,
         flat_key,
@@ -709,9 +804,12 @@
         w_gate,
         w_up,
         w_down,
-        tail_send,
-    )
-    old_tails = tail_back.reshape(all_slots, 2, page_size, local_width)[target]
+        kernel_tails,
+    )
+    for at, shift in enumerate(kernel_shifts):
+        tail_parts[shift] = tail_back[at]
+    tail_at = ((my_col - holder) % peer_count) * slot_count + slot_rank
+    old_tails = jnp.concatenate([tail_parts[i] for i in range(peer_count)], axis=0)[tail_at]
     hit_row = (jnp.arange(page_size)[None, :] == (dec_len % page_size)[:, None])[:, None, :, None]
     new_rows = jnp.stack([flat_key[pre_len:], flat_value[pre_len:]], axis=1)[:, :, None, :]
     tail_pages = jnp.where(hit_row, new_rows, old_tails)

time: 177 us -> 191 us (1.079); the launches traced: 175 us -> 191 us
  Pallas kernels: 143 us -> 112 us
  waiting for transfers between devices: 0.01 us -> 26.4 us
  local copies, waits for them, and re-layouts: 12.3 us -> 22.1 us
  starting transfers between devices: 5.72 us -> 13.4 us
  other arithmetic: 8.85 us -> 11.3 us
    pallas_call x1, Pallas kernels: 118 us -> 86.6 us  [rest_of_layer(): pl.pallas_call(functools.partial(layer_kernel, dims), out_shape=[jax.Shap...]
    ppermute x0 -> x5, waiting for transfers between devices: none -> 26.3 us  [on_device(): lax.ppermute(tail_send[shift], 'col', [(source, (source + shift) % peer_c...]
    ppermute x0 -> x5, starting transfers between devices: none -> 7.72 us  [on_device(): lax.ppermute(tail_send[shift], 'col', [(source, (source + shift) % peer_c...]
    unnamed x40 -> x56, local copies, waits for them, and re-layouts: 2.76 us -> 7.69 us
    slice x2, local copies, waits for them, and re-layouts: 0.15 us -> 2.83 us  [the longest x1 2.75 us: on_device(): tail_send[shift]]
    gather x2 -> x3, local copies, waits for them, and re-layouts: 6.56 us -> 7.16 us  [the longest x1 4.19 us: on_device(): kv_pool[last_page.reshape(peer_count, slot_count)[shift_peer].reshape(-1)]]
  transfers between devices with their start and end apart: 1 -> 6, of which waited for: 0 -> 3; matrix products, arithmetic and copies ran while one was open for 6% -> 10% of each run, Pallas kernels for 15% -> 59%
where the time goes in v3:
time: 191 us
  Pallas kernels  112 us (59%)
  waiting for transfers between devices  26.4 us (14%)
  local copies, waits for them, and re-layouts  22.1 us (12%)
  starting transfers between devices  13.4 us (7%)
  other arithmetic  11.3 us (6%)
  matrix products  4.53 us (2%)
    pallas_call x1, Pallas kernels, rest_of_layer(): pl.pallas_call(functools.partial(layer_kernel, dims), out_shape=[jax.Shap...  86.6 us
    ppermute x5, waiting for transfers between devices, on_device(): lax.ppermute(tail_send[shift], 'col', [(source, (source + shift) % peer_c...  26.3 us
    pallas_call x1, Pallas kernels, gather_all(): pl.pallas_call(functools.partial(gather_kernel, by_rows, n_col, n_row), o...  25.4 us
    ppermute x5, starting transfers between devices, on_device(): lax.ppermute(tail_send[shift], 'col', [(source, (source + shift) % peer_c...  7.72 us
    unnamed x56, local copies, waits for them, and re-layouts  7.69 us
    all_to_all x1, starting transfers between devices, on_device(): lax.all_to_all(send_int, 'col', split_axis=0, concat_axis=0, tiled=True)  5.72 us
    gather x1, local copies, waits for them, and re-layouts, on_device(): kv_pool[last_page.reshape(peer_count, slot_count)[shift_peer].reshape(-1)]  4.19 us
  transfers between devices with their start and end apart: 6, of which 3 were waited for; matrix products, arithmetic and copies ran while one was open for 10% of the time, Pallas kernels for 59%

profile of v3, /device:TPU:9, one launch (start us, length us, event | category | flops | bytes accessed | tf_op | source)
XLA Modules:
  0.0 190.9 jit_solution(7859333459329875480)
XLA Ops:
  0.6 0.7 fusion.11
  1.4 0.8 select_reduce_fusion.1
  2.9 0.7 pad_add_fusion
  4.6 5.7 %all-to-all-start = ((s32[8,2,10]{2,1,0:T(2,128)}), s32[8,2,10]{2,1,0:T(2,128)S(1)}, u32[]{:S(2)}, u32[]{:S(2)}) async-start(s32[8,2,10]{2,1,0:T(2,128)} %bitcast.13), calls=%async_computation | async-start | bytes 16384 | tf_op jit(solution)/shard_map/all_to_all | solution.py:700
  10.3 0.8 mul.212
  11.1 25.4 %gather_all.1 = (bf16[528,1024]{1,0:T(8,128)(2,1)}, bf16[1024,256]{1,0:T(8,128)(2,1)}, bf16[1024,256]{1,0:T(8,128)(2,1)}, bf16[1024,256]{1,0:T(8,128)(2,1)}, bf16[256,1024]{1,0:T(8,128)(2,1)}) custom-call(bf16[528,256]{1,0:T(8,128)(2,1)} %refs_14_.1, bf16[128,256]{1,0:T(8,128)(2,1)} %refs_1_.1, bf16[128,256]{1,0:T(8,128)(2,1)} %refs_2_.1, ...), custom_call_target="tpu_custom_call" | custom-call | bytes 80000000 | tf_op jit(solution)/shard_map/gather_all/pallas_call | solution.py:207
  36.6 1.7 fusion
  38.2 2.1 %multiply_reduce_fusion = (f32[528,4]{0,1:T(4,128)S(1)}, f32[528,256]{0,1:T(8,128)S(1)}) fusion(bf16[1024,256]{1,0:T(8,128)(2,1)} %get-tuple-element.12, bf16[528,1024]{1,0:T(8,128)(2,1)} %get-tuple-element.10, f32[1024]{0:T(1024)} %param.30, f32[528]{0:T(1024)S(1)} %add_rsqrt_fusion.2), kind=kOutput, calls=%fused_computation.13 | convolution fusion | flops 279254976 | bytes 2160960 | tf_op jit(solution)/shard_map/dot_general | solution.py:727
  41.3 0.7 multiply_reduce_fusion.1
  43.4 1.5 convolution_convert_fusion.refs_3_
  48.6 1.1 copy.104
  51.5 4.2 %gather_fusion.1 = bf16[16,2,128,256]{3,2,1,0:T(8,128)(2,1)} fusion(bf16[32,2,128,256]{3,2,1,0:T(8,128)(2,1)} %refs_11_.1, s32[1024]{0:T(1024)S(1)} %pad_clamp_fusion.1), kind=kCustom, calls=%fused_computation.1 | custom fusion | bytes 4194368 | tf_op jit(solution)/shard_map/gather | solution.py:709
  55.8 2.8 %fusion.23 = (bf16[2,2,128,256]{3,2,1,0:T(8,128)(2,1)}, bf16[2,2,128,256]{3,2,1,0:T(8,128)(2,1)}, bf16[2,2,128,256]{3,2,1,0:T(8,128)(2,1)}, bf16[2,2,128,256]{3,...) fusion(bf16[16,2,128,256]{3,2,1,0:T(8,128)(2,1)} %gather_fusion.1), kind=kLoop, calls=%fused_computation.105 | loop fusion | bytes 4194304 | tf_op jit(solution)/shard_map/slice | solution.py:717
  58.5 1.3 collective-permute-start
  59.8 0.8 pad_maximum_fusion.refs_20_
  60.8 86.6 %rest_of_layer.1 = (bf16[528,256]{1,0:T(8,128)(2,1)S(1)}, bf16[2,2,2,128,256]{4,3,2,1,0:T(8,128)(2,1)S(1)}) custom-call(f32[2,4]{1,0:T(2,128)S(1)} %pad_maximum_fusion.3.refs_0_, bf16[528,256]{1,0:T(8,128)(2,1)S(1)} %copy.95.refs_1_, bf16[528,256]{1,0:T(8,128)(2,1)S(1)} %copy.96.refs_2_, bf16[528,256]{1,0:T(8,128)(2,1)S(1)} %convolution_convert_fusion.refs_3_, ...), custom_call_target="tpu_custom_call" | custom-call | flops 199999995904 | bytes 200000000 | tf_op jit(solution)/shard_map/rest_of_layer/pallas_call | solution.py:616
  147.4 1.5 collective-permute-start.1
  148.9 1.0 collective-permute-start.2
  149.9 1.9 %collective-permute-start.3 = (bf16[2,2,128,256]{3,2,1,0:T(8,128)(2,1)S(1)}, bf16[2,2,128,256]{3,2,1,0:T(8,128)(2,1)S(1)}, u32[]{:S(2)}, u32[]{:S(2)}) collective-permute-start(bf16[2,2,128,256]{3,2,1,0:T(8,128)(2,1)S(1)} %copy-done.11), channel_id=1, source_target_pairs={{0,5},{1,6},{2,7},{3,0},{4,1},{5,2},{6,3},{7,4},{8,13},{9,14},{10,... | collective-permute-start | bytes 786440 | tf_op jit(solution)/shard_map/ppermute | solution.py:716
  151.8 2.0 %collective-permute-start.4 = (bf16[2,2,128,256]{3,2,1,0:T(8,128)(2,1)S(1)}, bf16[2,2,128,256]{3,2,1,0:T(8,128)(2,1)S(1)}, u32[]{:S(2)}, u32[]{:S(2)}) collective-permute-start(bf16[2,2,128,256]{3,2,1,0:T(8,128)(2,1)S(1)} %copy-done.10), channel_id=1, source_target_pairs={{0,6},{1,7},{2,0},{3,1},{4,2},{5,3},{6,4},{7,5},{8,14},{9,15},{10,... | collective-permute-start | bytes 786440 | tf_op jit(solution)/shard_map/ppermute | solution.py:716
  153.8 0.7 bitcast_dynamic-update-slice_fusion.1
  154.5 1.7 constant_dynamic-update-slice_fusion.4
  156.2 0.7 constant_dynamic-update-slice_fusion.3
  156.9 18.8 %collective-permute-done.2 = bf16[2,2,128,256]{3,2,1,0:T(8,128)(2,1)S(1)} collective-permute-done((bf16[2,2,128,256]{3,2,1,0:T(8,128)(2,1)S(1)}, bf16[2,2,128,256]{3,2,1,0:T(8,128)(2,1)S(1)}, u32[]{:S(2)}, u32[]{:S(2)}) %collective-permute-start.2) | collective-permute-done | bytes 262176 | tf_op jit(solution)/shard_map/ppermute | solution.py:716
  175.7 0.7 constant_dynamic-update-slice_fusion.2
  176.5 4.9 %collective-permute-done.3 = bf16[2,2,128,256]{3,2,1,0:T(8,128)(2,1)S(1)} collective-permute-done((bf16[2,2,128,256]{3,2,1,0:T(8,128)(2,1)S(1)}, bf16[2,2,128,256]{3,2,1,0:T(8,128)(2,1)S(1)}, u32[]{:S(2)}, u32[]{:S(2)}) %collective-permute-start.3) | collective-permute-done | bytes 262176 | tf_op jit(solution)/shard_map/ppermute | solution.py:716
  181.3 0.7 constant_dynamic-update-slice_fusion.1
  182.1 2.7 %collective-permute-done.4 = bf16[2,2,128,256]{3,2,1,0:T(8,128)(2,1)S(1)} collective-permute-done((bf16[2,2,128,256]{3,2,1,0:T(8,128)(2,1)S(1)}, bf16[2,2,128,256]{3,2,1,0:T(8,128)(2,1)S(1)}, u32[]{:S(2)}, u32[]{:S(2)}) %collective-permute-start.4) | collective-permute-done | bytes 262176 | tf_op jit(solution)/shard_map/ppermute | solution.py:716
  184.7 0.7 constant_dynamic-update-slice_fusion
  185.4 0.7 bitcast_dynamic-update-slice_fusion
  186.2 2.4 %gather_fusion.2 = bf16[16,2,128,256]{3,2,1,0:T(8,128)(2,1)S(1)} fusion(bf16[16,2,128,256]{3,2,1,0:T(8,128)(2,1)} %bitcast_dynamic-update-slice_fusion, s32[1024]{0:T(1024)} %pad_clamp_fusion), kind=kCustom, calls=%fused_computation.2 | custom fusion | bytes 4194368 | tf_op jit(solution)/shard_map/gather | solution.py:812
  188.6 1.5 broadcast_select_fusion
  (122 shorter events, 10.0 us)
Async XLA Ops:
  4.6 45.7 %all-to-all-start = ((s32[8,2,10]{2,1,0:T(2,128)}), s32[8,2,10]{2,1,0:T(2,128)S(1)}, u32[]{:S(2)}, u32[]{:S(2)}) async-start(s32[8,2,10]{2,1,0:T(2,128)} %bitcast.13), calls=%async_computation | async-start | bytes 16384 | tf_op jit(solution)/shard_map/all_to_all | solution.py:700
  36.5 3.9 %copy-start.1 = (s32[1,512]{1,0:T(1,128)S(1)}, s32[1,512]{1,0:T(1,128)}, u32[]{:S(2)}) copy-start(s32[1,512]{1,0:T(1,128)} %refs_5_.1) | copy-start | bytes 6148
  36.5 4.7 %copy-start.19 = (s32[16]{0:T(128)S(1)}, s32[16]{0:T(128)}, u32[]{:S(2)}) copy-start(s32[16]{0:T(128)} %param.39) | copy-start | bytes 196
  36.5 4.7 %copy-start.20 = (f32[256]{0:T(256)S(1)}, f32[256]{0:T(256)}, u32[]{:S(2)}) copy-start(f32[256]{0:T(256)} %param.32) | copy-start | bytes 3076
  36.5 4.7 %copy-start.9 = (bf16[528,1024]{1,0:T(8,128)(2,1)S(1)}, bf16[528,1024]{1,0:T(8,128)(2,1)}, u32[]{:S(2)}) copy-start(bf16[528,1024]{1,0:T(8,128)(2,1)} %get-tuple-element.10) | copy-start | bytes 3244036
  36.6 4.7 %copy-start.21 = (bf16[1024,256]{1,0:T(8,128)(2,1)S(1)}, bf16[1024,256]{1,0:T(8,128)(2,1)}, u32[]{:S(2)}) copy-start(bf16[1024,256]{1,0:T(8,128)(2,1)} %get-tuple-element.11) | copy-start | bytes 1572868
  36.6 4.7 %copy-start.22 = (f32[1024]{0:T(1024)S(1)}, f32[1024]{0:T(1024)}, u32[]{:S(2)}) copy-start(f32[1024]{0:T(1024)} %param.30) | copy-start | bytes 12292
  42.7 0.7 copy-start.16
  43.0 2.2 %copy-start.17 = (f32[4]{0:T(128)S(1)}, f32[4]{0:T(128)}, u32[]{:S(2)}) copy-start(f32[4]{0:T(128)} %param.34) | copy-start | bytes 52
  43.0 2.1 %copy-start.18 = (f32[4]{0:T(128)S(1)}, f32[4]{0:T(128)}, u32[]{:S(2)}) copy-start(f32[4]{0:T(128)} %param.35) | copy-start | bytes 52
  55.7 5.0 %copy-start = (bf16[528,256]{1,0:T(8,128)(2,1)S(1)}, bf16[528,256]{1,0:T(8,128)(2,1)}, u32[]{:S(2)}) copy-start(bf16[528,256]{1,0:T(8,128)(2,1)} %refs_14_.1) | copy-start | bytes 811012
  55.7 5.0 %copy-start.2 = (bf16[256,1024]{1,0:T(8,128)(2,1)S(1)}, bf16[256,1024]{1,0:T(8,128)(2,1)}, u32[]{:S(2)}) copy-start(bf16[256,1024]{1,0:T(8,128)(2,1)} %get-tuple-element.14.refs_16_) | copy-start | bytes 1572868
  55.7 5.0 %copy-start.3 = (bf16[128,1024]{1,0:T(8,128)(2,1)S(1)}, bf16[128,1024]{1,0:T(8,128)(2,1)}, u32[]{:S(2)}) copy-start(bf16[128,1024]{1,0:T(8,128)(2,1)} %refs_17_.1) | copy-start | bytes 786436
  55.7 5.0 %copy-start.4 = (bf16[128,1024]{1,0:T(8,128)(2,1)S(1)}, bf16[128,1024]{1,0:T(8,128)(2,1)}, u32[]{:S(2)}) copy-start(bf16[128,1024]{1,0:T(8,128)(2,1)} %refs_18_.1) | copy-start | bytes 786436
  55.7 5.0 %copy-start.5 = (bf16[1024,128]{1,0:T(8,128)(2,1)S(1)}, bf16[1024,128]{1,0:T(8,128)(2,1)}, u32[]{:S(2)}) copy-start(bf16[1024,128]{1,0:T(8,128)(2,1)} %refs_19_.1) | copy-start | bytes 786436
  55.7 5.0 %copy-start.6 = (s32[32,128]{1,0:T(8,128)S(1)}, s32[32,128]{1,0:T(8,128)}, u32[]{:S(2)}) copy-start(s32[32,128]{1,0:T(8,128)} %refs_10_.1) | copy-start | bytes 49156
  55.7 5.0 %copy-start.7 = (f32[1024]{0:T(1024)S(1)}, f32[1024]{0:T(1024)}, u32[]{:S(2)}) copy-start(f32[1024]{0:T(1024)} %param.31) | copy-start | bytes 12292
  55.7 5.0 %copy-start.8 = (s32[1,512]{1,0:T(1,128)S(1)}, s32[1,512]{1,0:T(1,128)}, u32[]{:S(2)}) copy-start(s32[1,512]{1,0:T(1,128)} %refs_6_.1) | copy-start | bytes 6148
  58.5 96.0 %collective-permute-start = (bf16[2,2,128,256]{3,2,1,0:T(8,128)(2,1)}, bf16[2,2,128,256]{3,2,1,0:T(8,128)(2,1)}, u32[]{:S(2)}, u32[]{:S(2)}) collective-permute-start(bf16[2,2,128,256]{3,2,1,0:T(8,128)(2,1)} %get-tuple-element.33), channel_id=1, source_target_pairs={{0,2},{1,3},{2,4},{3,5},{4,6},{5,7},{6,0},{7,1},{8,10},{9,11},{10,... | collective-permute-start | bytes 786440 | tf_op jit(solution)/shard_map/ppermute | solution.py:716
  60.8 86.6 %copy-start.13 = (bf16[2,2,128,256]{3,2,1,0:T(8,128)(2,1)S(1)}, bf16[2,2,128,256]{3,2,1,0:T(8,128)(2,1)}, u32[]{:S(2)}) copy-start(bf16[2,2,128,256]{3,2,1,0:T(8,128)(2,1)} %get-tuple-element.32) | copy-start | bytes 786436
  60.8 88.1 %copy-start.12 = (bf16[2,2,128,256]{3,2,1,0:T(8,128)(2,1)S(1)}, bf16[2,2,128,256]{3,2,1,0:T(8,128)(2,1)}, u32[]{:S(2)}) copy-start(bf16[2,2,128,256]{3,2,1,0:T(8,128)(2,1)} %get-tuple-element.31) | copy-start | bytes 786436
  60.8 89.1 %copy-start.11 = (bf16[2,2,128,256]{3,2,1,0:T(8,128)(2,1)S(1)}, bf16[2,2,128,256]{3,2,1,0:T(8,128)(2,1)}, u32[]{:S(2)}) copy-start(bf16[2,2,128,256]{3,2,1,0:T(8,128)(2,1)} %get-tuple-element.30) | copy-start | bytes 786436
  60.8 91.0 %copy-start.10 = (bf16[2,2,128,256]{3,2,1,0:T(8,128)(2,1)S(1)}, bf16[2,2,128,256]{3,2,1,0:T(8,128)(2,1)}, u32[]{:S(2)}) copy-start(bf16[2,2,128,256]{3,2,1,0:T(8,128)(2,1)} %get-tuple-element.29) | copy-start | bytes 786436
  147.4 8.8 %collective-permute-start.1 = (bf16[2,2,128,256]{3,2,1,0:T(8,128)(2,1)S(1)}, bf16[2,2,128,256]{3,2,1,0:T(8,128)(2,1)S(1)}, u32[]{:S(2)}, u32[]{:S(2)}) collective-permute-start(bf16[2,2,128,256]{3,2,1,0:T(8,128)(2,1)S(1)} %copy-done.13), channel_id=1, source_target_pairs={{0,3},{1,4},{2,5},{3,6},{4,7},{5,0},{6,1},{7,2},{8,11},{9,12},{10,... | collective-permute-start | bytes 786440 | tf_op jit(solution)/shard_map/ppermute | solution.py:716
  148.9 26.8 %collective-permute-start.2 = (bf16[2,2,128,256]{3,2,1,0:T(8,128)(2,1)S(1)}, bf16[2,2,128,256]{3,2,1,0:T(8,128)(2,1)S(1)}, u32[]{:S(2)}, u32[]{:S(2)}) collective-permute-start(bf16[2,2,128,256]{3,2,1,0:T(8,128)(2,1)S(1)} %copy-done.12), channel_id=1, source_target_pairs={{0,4},{1,5},{2,6},{3,7},{4,0},{5,1},{6,2},{7,3},{8,12},{9,13},{10,... | collective-permute-start | bytes 786440 | tf_op jit(solution)/shard_map/ppermute | solution.py:716
  149.9 31.5 %collective-permute-start.3 = (bf16[2,2,128,256]{3,2,1,0:T(8,128)(2,1)S(1)}, bf16[2,2,128,256]{3,2,1,0:T(8,128)(2,1)S(1)}, u32[]{:S(2)}, u32[]{:S(2)}) collective-permute-start(bf16[2,2,128,256]{3,2,1,0:T(8,128)(2,1)S(1)} %copy-done.11), channel_id=1, source_target_pairs={{0,5},{1,6},{2,7},{3,0},{4,1},{5,2},{6,3},{7,4},{8,13},{9,14},{10,... | collective-permute-start | bytes 786440 | tf_op jit(solution)/shard_map/ppermute | solution.py:716
  151.8 32.9 %collective-permute-start.4 = (bf16[2,2,128,256]{3,2,1,0:T(8,128)(2,1)S(1)}, bf16[2,2,128,256]{3,2,1,0:T(8,128)(2,1)S(1)}, u32[]{:S(2)}, u32[]{:S(2)}) collective-permute-start(bf16[2,2,128,256]{3,2,1,0:T(8,128)(2,1)S(1)} %copy-done.10), channel_id=1, source_target_pairs={{0,6},{1,7},{2,0},{3,1},{4,2},{5,3},{6,4},{7,5},{8,14},{9,15},{10,... | collective-permute-start | bytes 786440 | tf_op jit(solution)/shard_map/ppermute | solution.py:716
  186.2 2.4 %copy-start.14 = (bf16[16,2,256]{2,1,0:T(2,128)(2,1)S(1)}, bf16[16,2,256]{2,1,0:T(2,128)(2,1)}, u32[]{:S(2)}) copy-start(bf16[16,2,256]{2,1,0:T(2,128)(2,1)} %copy.101) | copy-start | bytes 49156
  186.2 2.4 %copy-start.15 = (pred[16,128]{1,0:T(8,128)(4,1)S(1)}, pred[16,128]{1,0:T(8,128)(4,1)}, u32[]{:S(2)}) copy-start(pred[16,128]{1,0:T(8,128)(4,1)} %iota_compare_fusion) | copy-start | bytes 6148

commit v4 on v3

--- a/solution.py
+++ b/solution.py
@@ -11,27 +11,6 @@
 
 
 eps = 1e-05
-
-
-def norm_rows(values, gain_row):
-    return values * lax.rsqrt(jnp.mean(values * values, axis=-1, keepdims=True) + eps) * gain_row
-
-
-def rotate(tensor, places):
-    half_size = tensor.shape[-1] // 2
-    spacing = jnp.arange(half_size).astype(jnp.float32) * (2.0 / tensor.shape[-1])
-    angles = places.astype(jnp.float32)[:, None] * jnp.power(10000.0, -spacing)[None, :]
-    cosine = jnp.cos(angles)[:, None, :]
-    sine_part = jnp.sin(angles)[:, None, :]
-    lower_half = tensor[..., :half_size]
-    upper_half = tensor[..., half_size:]
-    return jnp.concatenate(
-        [
-            lower_half * cosine - upper_half * sine_part,
-            upper_half * cosine + lower_half * sine_part,
-        ],
-        axis=-1,
-    )
 
 
 def segment_time(variates):
@@ -145,84 +124,6 @@
     return (depth, width * n_col)
 
 
-def gather_kernel(by_rows, n_col, n_row, *refs):
-    count = len(by_rows)
-    x_ref = refs[0]
-    shards = refs[1 : 1 + count]
-    x_out = refs[1 + count]
-    wholes = refs[2 + count : 2 + 2 * count]
-    own_sem, x_send, x_recv = refs[2 + 2 * count : 5 + 2 * count]
-    my_row = lax.axis_index("row")
-    half_way = n_col // 2
-    greet(n_col, n_row)
-    hop, own_copy = ring_hops(by_rows, n_col, shards, wholes, refs[5 + 2 * count :])
-    width = x_ref.shape[1]
-    x_place = x_out.at[:, pl.ds(pl.multiple_of(my_row * width, 128), width)]
-
-    def x_copy(step):
-        return pltpu.make_async_remote_copy(
-            src_ref=x_ref,
-            dst_ref=x_place,
-            send_sem=x_send.at[step],
-            recv_sem=x_recv.at[step],
-            device_id={"row": (my_row + step) % n_row},
-            device_id_type=pl.DeviceIdType.MESH,
-        )
-
-    own = [own_copy(i, own_sem.at[i]) for i in range(count)]
-    own.append(pltpu.make_async_copy(x_ref, x_place, own_sem.at[count]))
-    for index in range(count):
-        hop(index, 0, True).start()
-        hop(index, 0, False).start()
-    for step in range(1, n_row):
-        x_copy(step).start()
-    for copy in own:
-        copy.start()
-    for step in range(half_way):
-        for index in range(count):
-            for to_right in (True, False):
-                hop(index, step, to_right).wait_recv()
-                if step + 1 < half_way:
-                    hop(index, step + 1, to_right).start()
-    for step in range(half_way):
-        for index in range(count):
-            for to_right in (True, False):
-                hop(index, step, to_right).wait_send()
-    for step in range(1, n_row):
-        x_copy(step).wait()
-    for copy in own:
-        copy.wait()
-
-
-def gather_all(layer_input, shards, by_rows):
-    n_col, n_row = lax.axis_size("col"), lax.axis_size("row")
-    count = len(shards)
-    half_way = n_col // 2
-    shapes = [
-        jax.ShapeDtypeStruct((layer_input.shape[0], layer_input.shape[1] * n_row), jnp.bfloat16)
-    ] + [
-        jax.ShapeDtypeStruct(whole_shape(shard, rows, n_col), jnp.bfloat16)
-        for shard, rows in zip(shards, by_rows)
-    ]
-    return pl.pallas_call(
-        functools.partial(gather_kernel, by_rows, n_col, n_row),
-        out_shape=shapes,
-        in_specs=[pl.BlockSpec(memory_space=pl.ANY)] * (1 + count),
-        out_specs=[pl.BlockSpec(memory_space=pl.ANY)] * (1 + count),
-        scratch_shapes=[
-            pltpu.SemaphoreType.DMA((count + 1,)),
-            pltpu.SemaphoreType.DMA((n_row,)),
-            pltpu.SemaphoreType.DMA((n_row,)),
-        ]
-        + [pltpu.SemaphoreType.DMA((count, half_way))] * 4,
-        compiler_params=pltpu.CompilerParams(collective_id=0, has_side_effects=True),
-        cost_estimate=pl.CostEstimate(
-            flops=0, bytes_accessed=80_000_000, transcendentals=0
-        ),
-        name="gather_all",
-    )(layer_input, *shards)
-
-
 NT = (((1,), (1,)), ((), ()))
 
 
@@ -234,34 +135,47 @@
 
 
 def layer_kernel(dims, *refs):
-    n_col, n_row, heads, dec_count, page_count, score_scale, tail_shifts = dims
+    n_col, n_row, heads, dec_count, page_count, score_scale, slot_count = dims
     (
         bias_ref,
-        q_ref,
-        k_ref,
-        v_ref,
+        page_ref,
         var_col,
         var_row,
         keep_row,
-        ask_ref,
         facts_ref,
         slot_bias,
+        lane_bias,
         page_var,
-        pool_ref,
         pick_ref,
-        own_ref,
+        place_ref,
+        cos_ref,
+        sin_ref,
+        gain_ref,
+        norm_ref,
         x_ref,
-        norm_ref,
-        wo_ref,
+        pool_hbm,
+        wq_shard,
+        wk_shard,
+        wv_shard,
+        wo_shard,
         wg_shard,
         wu_shard,
         wd_shard,
-        tail_ref,
         hidden_ref,
+        k_ref,
+        v_ref,
         tail_out,
+        wq_ref,
+        wk_ref,
+        wv_ref,
+        wo_ref,
         wg_ref,
         wu_ref,
         wd_ref,
+        pool_ref,
+        tail_ref,
+        q_ref,
+        ask_ref,
         asked,
         answer,
         answered,
@@ -270,6 +184,7 @@
         pair_recv,
         sum_send,
         sum_recv,
+        x_all,
         resid_all,
         normed,
         units,
@@ -300,10 +215,10 @@
     pre_len = rows - dec_count
     greet(n_col, n_row)
     hop, own_copy = ring_hops(
-        (True, True, False),
+        (True, True, True, False, True, True, False),
         n_col,
-        (wg_shard, wu_shard, wd_shard),
-        (wg_ref, wu_ref, wd_ref),
+        (wq_shard, wk_shard, wv_shard, wo_shard, wg_shard, wu_shard, wd_shard),
+        (wq_ref, wk_ref, wv_ref, wo_ref, wg_ref, wu_ref, wd_ref),
         (r_send, r_recv, l_send, l_recv),
     )
 
@@ -327,15 +242,8 @@
             answer.at[(me + step) % n_col], answered.at[me], ans_send, ans_recv, step
         )
 
-    def tail(at):
-        return pltpu.make_async_remote_copy(
-            src_ref=tail_ref.at[at],
-            dst_ref=tail_out.at[at],
-            send_sem=t_send.at[at],
-            recv_sem=t_recv.at[at],
-            device_id={"col": (me + tail_shifts[at]) % n_col},
-            device_id_type=pl.DeviceIdType.MESH,
-        )
+    def tail(step):
+        return to_peer(tail_ref.at[step], tail_out.at[step], t_send, t_recv, step)
 
     chips = n_row // 2
     chip, core = my_row // 2, my_row % 2
@@ -373,24 +281,49 @@
             there * 2 + core,
         )
 
-    def far(step):
+    def far(stage, step):
+        held = (x_all, resid_all)[stage].at[my_row]
         return to_row(
-            resid_all.at[my_row],
-            resid_all.at[my_row],
-            far_send_sem.at[step],
-            far_recv_sem.at[step],
+            held,
+            held,
+            far_send_sem.at[stage, step],
+            far_recv_sem.at[stage, step],
             chip_at(step) * 2 + core,
         )
 
-    def near(step):
-        held = ((chip + chips - step) % chips) * 2 + core
+    def near(stage, step):
+        held = (x_all, resid_all)[stage].at[((chip + chips - step) % chips) * 2 + core]
         return to_row(
-            resid_all.at[held],
-            resid_all.at[held],
-            near_send_sem.at[step],
-            near_recv_sem.at[step],
+            held,
+            held,
+            near_send_sem.at[stage, step],
+            near_recv_sem.at[stage, step],
             chip * 2 + 1 - core,
         )
+
+    def share_start(stage):
+        for step in range(1, chips):
+            far(stage, step).start()
+        near(stage, 0).start()
+
+    def share_end(stage):
+        for step in range(1, chips):
+            far(stage, step).wait_recv()
+            near(stage, step).start()
+        for step in range(chips):
+            near(stage, step).wait_recv()
+
+    def norm_all(held, which):
+        squares = jnp.zeros((rows, 1), jnp.float32)
+        for piece in range(n_row):
+            values = held[piece].astype(jnp.float32)
+            squares = squares + jnp.sum(values * values, axis=1, keepdims=True)
+        scale = lax.rsqrt(squares * (1.0 / (n_row * width)) + eps)
+        for piece in range(n_row):
+            cols = slice(piece * width, (piece + 1) * width)
+            normed[:, cols] = (
+                held[piece].astype(jnp.float32) * scale * norm_ref[which : which + 1, cols]
+            ).astype(jnp.bfloat16)
 
     def reduce_start(stage, left, weight):
         def product(target):
@@ -420,22 +353,81 @@
             total_share = total_share + sum_recv[stage, there].astype(jnp.float32)
         return total_share
 
-    def pump(step):
-        for index in range(3):
+    early, late = (0, 1, 2), (3, 4, 5, 6)
+
+    def begin(index):
+        hop(index, 0, True).start()
+        hop(index, 0, False).start()
+        own_copy(index, own_sem.at[index]).start()
+
+    def pump(group, step):
+        for index in group:
             for to_right in (True, False):
                 hop(index, step, to_right).wait_recv()
                 if step + 1 < half_way:
                     hop(index, step + 1, to_right).start()
 
-    own_ask = pltpu.make_async_copy(ask_ref.at[me], asked.at[me], own_sem.at[3])
+    own_ask = pltpu.make_async_copy(ask_ref.at[me], asked.at[me], own_sem.at[7])
+    own_tail = pltpu.make_async_copy(tail_ref.at[0], tail_out.at[0], own_sem.at[8])
+    pool_copy = pltpu.make_async_copy(pool_hbm, pool_ref, own_sem.at[10])
+    for index in early:
+        begin(index)
+    x_all[my_row] = x_ref[...]
+    share_start(0)
+    pool_copy.start()
+    pump(early, 0)
+    begin(3)
+    begin(4)
+    share_end(0)
+    norm_all(x_all, 0)
+    pump(early, 1)
+    pool_copy.wait()
+    for step in range(n_col):
+        for slot in range(slot_count):
+            tail_ref[step, slot] = pool_ref[page_ref[step * slot_count + slot]]
+    begin(5)
+    begin(6)
+    for step in range(2, half_way):
+        pump(early, step)
+    for index in early:
+        own_copy(index, own_sem.at[index]).wait()
+
+    row_lane = lax.broadcasted_iota(jnp.int32, (width, width), 0)
+    col_lane = lax.broadcasted_iota(jnp.int32, (width, width), 1)
+    same_head = jnp.where(row_lane // HD == col_lane // HD, 1.0, 0.0)
+    upper = col_lane % HD >= HD // 2
+    turn = jnp.where(upper & (row_lane == col_lane - HD // 2), 1.0, 0.0) - jnp.where(
+        jnp.logical_not(upper) & (row_lane == col_lane + HD // 2), 1.0, 0.0
+    )
+
+    def exact(left, right):
+        return jnp.dot(
+            left, right, preferred_element_type=jnp.float32, precision=lax.Precision.HIGHEST
+        )
+
+    def rotated(weight, which):
+        value = jnp.dot(normed[...], weight[...], preferred_element_type=jnp.float32)
+        square = exact(value * value, same_head) * (1.0 / HD)
+        value = value * lax.rsqrt(square + eps) * gain_ref[which : which + 1, :]
+        return (value * cos_ref[...] + exact(value, turn) * sin_ref[...]).astype(jnp.bfloat16)
+
+    q_ref[...] = rotated(wq_ref, 0)
+    slots, page_size = asked.shape[0] * asked.shape[1], pool_ref.shape[2]
+    slot_head = (lax.broadcasted_iota(jnp.int32, (slots, width), 0) % (slots // n_col)) % heads
+    mine = lax.broadcasted_iota(jnp.int32, (slots, width), 1) // HD == slot_head
+    sent = jnp.dot(place_ref[...], q_ref[pre_len:rows, :], preferred_element_type=jnp.float32)
+    ask_ref[...] = jnp.where(mine, sent, 0.0).reshape(n_col, slots // n_col, width)
     for step in range(1, n_col):
         ask(step).start()
     own_ask.start()
-    for index in range(3):
-        hop(index, 0, True).start()
-        hop(index, 0, False).start()
-    for index in range(3):
-        own_copy(index, own_sem.at[index]).start()
+    own_tail.start()
+    k_ref[...] = rotated(wk_ref, 1)
+    v_ref[...] = jnp.dot(normed[...], wv_ref[...], preferred_element_type=jnp.float32).astype(
+        jnp.bfloat16
+    )
+    pump(late, 0)
+    tail(1).start()
+    tail(n_col - 1).start()
 
     block = 128
     lane_head = lax.broadcasted_iota(jnp.int32, (block, width), 1) // HD
@@ -471,7 +463,6 @@
     own_ask.wait()
     for step in range(1, n_col):
         ask(step).wait_recv()
-    slots, page_size = asked.shape[0] * asked.shape[1], pool_ref.shape[2]
     queries = asked[...].reshape(slots, width).astype(jnp.bfloat16)
     facts = facts_ref[...]
     length = facts[:, page_count : page_count + 1]
@@ -510,17 +501,18 @@
     answer[:, :, width:] = jnp.broadcast_to(total, (slots, 128)).reshape(
         n_col, slots // n_col, 128
     )
-    own_reply = pltpu.make_async_copy(answer.at[me], answered.at[me], own_sem.at[5])
+    own_reply = pltpu.make_async_copy(answer.at[me], answered.at[me], own_sem.at[9])
     own_reply.start()
     for step in range(1, n_col):
         reply(step).start()
-    pump(0)
+    pump(late, 1)
+    if n_col > 4:
+        tail(2).start()
+        tail(n_col - 2).start()
     own_reply.wait()
     for step in range(1, n_col):
         reply(step).wait_recv()
     back = answered[...].reshape(slots, width + 128)
-    slot_head = (lax.broadcasted_iota(jnp.int32, (slots, width), 0) % (slots // n_col)) % heads
-    mine = lax.broadcasted_iota(jnp.int32, (slots, width), 1) // HD == slot_head
     pick = pick_ref[...]
     cached = jnp.dot(
         pick,
@@ -534,41 +526,36 @@
         preferred_element_type=jnp.float32,
         precision=lax.Precision.HIGHEST,
     )
-    own_exp = own_ref[...]
+    own_score = exact(
+        q_ref[pre_len:rows, :].astype(jnp.float32) * k_ref[pre_len:rows, :].astype(jnp.float32),
+        same_head,
+    )
+    own_exp = jnp.exp(own_score * score_scale + lane_bias[...])
     whole_total = cached_total + own_exp
     attended[pl.ds(pre_len, dec_count), :] = (
         cached * (cached_total / whole_total)
         + v_ref[pre_len:rows, :].astype(jnp.float32) * (own_exp / whole_total)
     ).astype(jnp.bfloat16)
 
+    own_copy(3, own_sem.at[3]).wait()
+    if half_way > 2:
+        pump((3,), 2)
+    for step in range(3, half_way):
+        pump((3,), step)
     resid[...] = reduce_start(0, attended, wo_ref) + x_ref[...].astype(jnp.float32)
-    pump(1)
+    if half_way > 2:
+        pump(late[1:], 2)
     total_share = reduce_end(0, resid[...])
     resid[...] = total_share
     resid_all[my_row] = total_share.astype(jnp.bfloat16)
-    for step in range(1, chips):
-        far(step).start()
-    near(0).start()
-    for step in range(2, half_way):
-        pump(step)
-    for at in range(len(tail_shifts)):
-        tail(at).start()
-    for step in range(1, chips):
-        far(step).wait_recv()
-        near(step).start()
-    for step in range(chips):
-        near(step).wait_recv()
-    squares = jnp.zeros((rows, 1), jnp.float32)
-    for piece in range(n_row):
-        values = resid_all[piece].astype(jnp.float32)
-        squares = squares + jnp.sum(values * values, axis=1, keepdims=True)
-    scale = lax.rsqrt(squares * (1.0 / (n_row * width)) + eps)
-    for piece in range(n_row):
-        cols = slice(piece * width, (piece + 1) * width)
-        normed[:, cols] = (
-            resid_all[piece].astype(jnp.float32) * scale * norm_ref[:, cols]
-        ).astype(jnp.bfloat16)
-    for index in range(3):
+    share_start(1)
+    for step in range(3, half_way):
+        pump(late[1:], step)
+    for step in range(3, n_col - 2):
+        tail(step).start()
+    share_end(1)
+    norm_all(resid_all, 1)
+    for index in late[1:]:
         own_copy(index, own_sem.at[index]).wait()
 
     tile = 256
@@ -583,75 +570,79 @@
     resid[...] = reduce_start(1, units, wd_ref) + resid[...]
     hidden_ref[...] = reduce_end(1, resid[...]).astype(jnp.bfloat16)
 
-    for at in range(len(tail_shifts)):
-        tail(at).wait()
     for step in range(chips):
         pair(0, step).wait_send()
         pair(1, step).wait_send()
-        near(step).wait_send()
+        near(0, step).wait_send()
+        near(1, step).wait_send()
     for step in range(1, chips):
         summed(0, step).wait_send()
         summed(1, step).wait_send()
-        far(step).wait_send()
+        far(0, step).wait_send()
+        far(1, step).wait_send()
     for step in range(1, n_col):
         ask(step).wait_send()
         reply(step).wait_send()
     for step in range(half_way):
-        for index in range(3):
+        for index in range(7):
             for to_right in (True, False):
                 hop(index, step, to_right).wait_send()
-
-
-def rest_of_layer(dims, *operands):
+    own_tail.wait()
+    for step in range(1, n_col):
+        tail(step).wait()
+
+
+def whole_layer(dims, operands, shards):
     n_col, n_row = dims[:2]
-    x, wg, wu, wd, tails = operands[14], operands[17], operands[18], operands[19], operands[20]
-    ask = operands[7]
+    slot_count = dims[6]
+    x, pool = operands[15], operands[16]
+    slot_rows = operands[5].shape[0] // n_col
     rows, width = x.shape
     half_way = n_col // 2
     chips = n_row // 2
-    full = n_row * width
     vmem = pl.BlockSpec(memory_space=pltpu.VMEM)
+    smem = pl.BlockSpec(memory_space=pltpu.SMEM)
     anywhere = pl.BlockSpec(memory_space=pl.ANY)
     dma = pltpu.SemaphoreType.DMA
+    tails = (n_col, slot_count) + pool.shape[1:]
+    by_rows = (True, True, True, False, True, True, False)
+    act = (rows, width)
     return pl.pallas_call(
         functools.partial(layer_kernel, dims),
-        out_shape=[
-            jax.ShapeDtypeStruct((rows, width), jnp.bfloat16),
-            jax.ShapeDtypeStruct(tails.shape, jnp.bfloat16),
-        ],
-        in_specs=[pl.BlockSpec(memory_space=pltpu.SMEM)] + [vmem] * 19 + [anywhere],
-        out_specs=[vmem, anywhere],
+        out_shape=[jax.ShapeDtypeStruct(act, jnp.bfloat16)] * 3
+        + [jax.ShapeDtypeStruct(tails, jnp.bfloat16)],
+        in_specs=[smem] * 2 + [vmem] * 14 + [anywhere] * 8,
+        out_specs=[vmem] * 3 + [anywhere],
         scratch_shapes=[
-            pltpu.VMEM(whole_shape(wg, True, n_col), jnp.bfloat16),
-            pltpu.VMEM(whole_shape(wu, True, n_col), jnp.bfloat16),
-            pltpu.VMEM(whole_shape(wd, False, n_col), jnp.bfloat16),
-            pltpu.VMEM(ask.shape, jnp.float32),
-            pltpu.VMEM(ask.shape[:2] + (width + 128,), jnp.float32),
-            pltpu.VMEM(ask.shape[:2] + (width + 128,), jnp.float32),
-            pltpu.VMEM((rows, width), jnp.bfloat16),
-            pltpu.VMEM((2, chips, rows, width), jnp.bfloat16),
-            pltpu.VMEM((2, chips, rows, width), jnp.bfloat16),
-            pltpu.VMEM((2, chips, rows, width), jnp.bfloat16),
-            pltpu.VMEM((2, chips, rows, width), jnp.bfloat16),
-            pltpu.VMEM((n_row, rows, width), jnp.bfloat16),
-            pltpu.VMEM((rows, full), jnp.bfloat16),
-            pltpu.VMEM((rows, wg.shape[1]), jnp.bfloat16),
-            pltpu.VMEM((rows, width), jnp.float32),
-            dma((6,)),
+            pltpu.VMEM(whole_shape(shard, along, n_col), jnp.bfloat16)
+            for shard, along in zip(shards, by_rows)
         ]
-        + [dma((n_col,))] * 4
-        + [dma((tails.shape[0],))] * 2
-        + [dma((2, chips))] * 4
-        + [dma((chips,))] * 4
-        + [dma((3, half_way))] * 4,
+        + [
+            pltpu.VMEM(pool.shape, jnp.bfloat16),
+            pltpu.VMEM(tails, jnp.bfloat16),
+            pltpu.VMEM(act, jnp.bfloat16),
+            pltpu.VMEM((n_col, slot_rows, width), jnp.float32),
+            pltpu.VMEM((n_col, slot_rows, width), jnp.float32),
+            pltpu.VMEM((n_col, slot_rows, width + 128), jnp.float32),
+            pltpu.VMEM((n_col, slot_rows, width + 128), jnp.float32),
+            pltpu.VMEM(act, jnp.bfloat16),
+        ]
+        + [pltpu.VMEM((2, chips) + act, jnp.bfloat16)] * 4
+        + [pltpu.VMEM((n_row,) + act, jnp.bfloat16)] * 2
+        + [
+            pltpu.VMEM((rows, n_row * width), jnp.bfloat16),
+            pltpu.VMEM((rows, shards[4].shape[1]), jnp.bfloat16),
+            pltpu.VMEM(act, jnp.float32),
+            dma((11,)),
+        ]
+        + [dma((n_col,))] * 6
+        + [dma((2, chips))] * 8
+        + [dma((7, half_way))] * 4,
         compiler_params=pltpu.CompilerParams(
-            collective_id=1, has_side_effects=True, vmem_limit_bytes=50 * 1024 * 1024
+            collective_id=0, has_side_effects=True, vmem_limit_bytes=56 * 1024 * 1024
         ),
-        cost_estimate=pl.CostEstimate(
-            flops=200_000_000_000, bytes_accessed=200_000_000, transcendentals=2_000_000
-        ),
-        name="rest_of_layer",
-    )(*operands)
+        name="whole_layer",
+    )(*operands, *shards)
 
 
 def on_device(
@@ -706,50 +697,23 @@
     last_page = jnp.sum(jnp.where(last_place, slot_table, 0), axis=1)
     my_col = lax.axis_index("col")
     shift_peer = (my_col + jnp.arange(peer_count)) % peer_count
-    tail_send = kv_pool[last_page.reshape(peer_count, slot_count)[shift_peer].reshape(-1)]
-    tail_send = tail_send.reshape(peer_count, slot_count, 2, page_size, local_width)
-    first_shift = max(peer_count // 2 - 2, 1)
-    last_shift = min(first_shift + 5, peer_count)
-    kernel_shifts = tuple(range(1, first_shift)) + tuple(range(last_shift, peer_count))
-    tail_parts = {0: tail_send[0]}
-    for shift in range(first_shift, last_shift):
-        tail_parts[shift] = lax.ppermute(
-            tail_send[shift],
-            "col",
-            [(source, (source + shift) % peer_count) for source in range(peer_count)],
-        )
-    kernel_tails = jnp.stack([tail_send[shift] for shift in kernel_shifts])
-    gathered_input, full_q, full_k, full_v, full_o = gather_all(
-        layer_input, (w_q, w_k, w_v, w_o), (True, True, True, False)
-    )
-    normed = norm_rows(gathered_input.astype(jnp.float32), norm1).astype(jnp.bfloat16)
-    queries = jnp.dot(normed, full_q, preferred_element_type=jnp.float32)
-    keys_proj = jnp.dot(normed, full_k, preferred_element_type=jnp.float32)
-    values_proj = jnp.dot(normed, full_v, preferred_element_type=jnp.float32)
-    places = jnp.concatenate([segment_time(pre_variate[0]), dec_len])
-    query_rot = rotate(
-        norm_rows(queries.reshape(row_count, heads_here, HD), q_gain.reshape(heads_here, HD)),
-        places,
-    ).astype(jnp.bfloat16)
-    key_rot = rotate(
-        norm_rows(keys_proj.reshape(row_count, heads_here, HD), k_gain.reshape(heads_here, HD)),
-        places,
-    ).astype(jnp.bfloat16)
-    value_bf = values_proj.astype(jnp.bfloat16).reshape(row_count, heads_here, HD)
-
-    flat_query = query_rot.reshape(row_count, local_width)
-    flat_key = key_rot.reshape(row_count, local_width)
-    flat_value = value_bf.reshape(row_count, local_width)
+    shift_page = jnp.sum(
+        jnp.where(
+            (shift_peer[:, None] == jnp.arange(peer_count)[None, :])[:, :, None],
+            last_page.reshape(1, peer_count, slot_count),
+            0,
+        ),
+        axis=1,
+    ).reshape(-1)
+
+    places = jnp.concatenate([segment_time(pre_variate[0]), dec_len]).astype(jnp.float32)
+    spacing = jnp.arange(HD // 2).astype(jnp.float32) * (2.0 / HD)
+    angles = places[:, None] * jnp.power(10000.0, -spacing)[None, :]
+    cosines = jnp.tile(jnp.cos(angles), (1, 2 * heads_here))
+    sines = jnp.tile(jnp.sin(angles), (1, 2 * heads_here))
 
     used_rows = slot_count * heads_here
     slot_rows = -(-used_rows // 8) * 8
-    sent_query = jnp.dot(
-        to_slot.astype(jnp.bfloat16), flat_query[pre_len:], preferred_element_type=jnp.float32
-    )
-    lane_head = jnp.arange(local_width) // HD
-    head_rows = (jnp.arange(heads_here)[:, None] == lane_head[None, :]).astype(jnp.float32)
-    ask = (sent_query[:, None, :] * head_rows[None]).reshape(peer_count, used_rows, local_width)
-    ask = jnp.pad(ask, ((0, 0), (0, slot_rows - used_rows), (0, 0)))
 
     def per_row(values):
         wide = jnp.broadcast_to(
@@ -765,16 +729,8 @@
         jnp.pad(jnp.tile(bias_pair, (slot_count, 1)), ((0, slot_rows - used_rows), (0, 0))),
         (peer_count, 1),
     )
-    pick = per_row(to_slot.astype(jnp.float32)).T
-    own_score = (
-        jnp.sum(
-            query_rot[pre_len:].astype(jnp.float32) * key_rot[pre_len:].astype(jnp.float32), axis=2
-        )
-        * score_scale
-        + bias_same[None]
-    )
-    own_exp = jnp.repeat(jnp.exp(own_score), HD, axis=1)
-    hidden, tail_back = rest_of_layer(
+    placed = per_row(to_slot.astype(jnp.float32))
+    hidden, flat_key, flat_value, tail_back = whole_layer(
         (
             peer_count,
             lax.axis_size("row"),
@@ -782,41 +738,38 @@
             dec_count,
             page_count,
             score_scale,
-            kernel_shifts,
+            slot_count,
         ),
-        jnp.stack([bias_same, bias_diff]),
-        flat_query,
-        flat_key,
-        flat_value,
-        pre_variate[0][:, None],
-        pre_variate,
-        pre_keep,
-        ask,
-        facts,
-        slot_bias,
-        page_variates,
-        kv_pool,
-        pick,
-        own_exp,
-        layer_input,
-        norm2[None],
-        full_o,
-        w_gate,
-        w_up,
-        w_down,
-        kernel_tails,
-    )
-    for at, shift in enumerate(kernel_shifts):
-        tail_parts[shift] = tail_back[at]
+        (
+            jnp.stack([bias_same, bias_diff]),
+            shift_page,
+            pre_variate[0][:, None],
+            pre_variate,
+            pre_keep,
+            facts,
+            slot_bias,
+            jnp.repeat(bias_same, HD)[None],
+            page_variates,
+            placed.T,
+            placed.astype(jnp.bfloat16),
+            cosines,
+            sines,
+            jnp.stack([q_gain, k_gain]),
+            jnp.stack([norm1, norm2]),
+            layer_input,
+            kv_pool,
+        ),
+        (w_q, w_k, w_v, w_o, w_gate, w_up, w_down),
+    )
     tail_at = ((my_col - holder) % peer_count) * slot_count + slot_rank
-    old_tails = jnp.concatenate([tail_parts[i] for i in range(peer_count)], axis=0)[tail_at]
+    old_tails = tail_back.reshape(all_slots, 2, page_size, local_width)[tail_at]
     hit_row = (jnp.arange(page_size)[None, :] == (dec_len % page_size)[:, None])[:, None, :, None]
     new_rows = jnp.stack([flat_key[pre_len:], flat_value[pre_len:]], axis=1)[:, :, None, :]
     tail_pages = jnp.where(hit_row, new_rows, old_tails)
     prefill_pages = jnp.stack(
         [
-            key_rot[:pre_len].reshape(pre_len // page_size, page_size, local_width),
-            value_bf[:pre_len].reshape(pre_len // page_size, page_size, local_width),
+            flat_key[:pre_len].reshape(pre_len // page_size, page_size, local_width),
+            flat_value[:pre_len].reshape(pre_len // page_size, page_size, local_width),
         ],
         axis=1,
     )

time: 191 us -> 186 us (0.974)
  Pallas kernels: 112 us -> 148 us
  waiting for transfers between devices: 26.4 us -> 0.01 us
  starting transfers between devices: 13.4 us -> 5.72 us
  local copies, waits for them, and re-layouts: 22.1 us -> 15.2 us
  matrix products: 4.53 us -> 0 us
  other arithmetic: 11.3 us -> 14.6 us
    pallas_call x2 -> x1, Pallas kernels: 112 us -> 148 us  [whole_layer(): pl.pallas_call(functools.partial(layer_kernel, dims), out_shape=[jax.Shap...]
    ppermute x5 -> x0, waiting for transfers between devices: 26.3 us -> none  [on_device(): lax.ppermute(tail_send[shift], 'col', [(source, (source + shift) % peer_c...]
    ppermute x5 -> x0, starting transfers between devices: 7.72 us -> none  [on_device(): lax.ppermute(tail_send[shift], 'col', [(source, (source + shift) % peer_c...]
    unnamed x56 -> x5, local copies, waits for them, and re-layouts: 7.69 us -> 1.54 us
    gather x3 -> x1, local copies, waits for them, and re-layouts: 7.16 us -> 2.27 us  [on_device(): old_tails = tail_back.reshape(all_slots, 2, page_size, local_width)[tail_at]]
    dot_general x4 -> x0, matrix products: 4.53 us -> none  [the longest x1 2.12 us: on_device(): keys_proj = jnp.dot(normed, full_k, preferred_element_type=jnp.float32)]
    another operation x3 -> x6, local copies, waits for them, and re-layouts: 0.36 us -> 2.89 us  [the longest x2 1.05 us: on_device(): sines = jnp.tile(jnp.sin(angles), (1, 2 * heads_here))]
    another operation x4 -> x5, other arithmetic: 1.55 us -> 3.78 us  [the longest x1 1.31 us: on_device(): jnp.stack([norm1, norm2])]
  transfers between devices with their start and end apart: 6 -> 1, of which waited for: 3 -> 0; matrix products, arithmetic and copies ran while one was open for 10% -> 9% of each run, Pallas kernels for 59% -> 0%
where the time goes in v4:
time: 186 us; the launch traced here: 185 us
  Pallas kernels  148 us (80%)
  local copies, waits for them, and re-layouts  15.2 us (8%)
  other arithmetic  14.6 us (8%)
  starting transfers between devices  5.72 us (3%)
    pallas_call x1, Pallas kernels, whole_layer(): pl.pallas_call(functools.partial(layer_kernel, dims), out_shape=[jax.Shap...  148 us
    all_to_all x1, starting transfers between devices, on_device(): lax.all_to_all(send_int, 'col', split_axis=0, concat_axis=0, tiled=True)  5.72 us
  transfers between devices with their start and end apart: 1, of which 0 were waited for; matrix products, arithmetic and copies ran while one was open for 9% of the time, Pallas kernels for 0%

profile of v4, /device:TPU:9, one launch (start us, length us, event | category | flops | bytes accessed | tf_op | source)
XLA Modules:
  0.0 184.7 jit_solution(7789096178960866615)
XLA Ops:
  0.6 0.7 fusion.7
  1.4 0.8 select_reduce_fusion.2
  2.2 0.7 multiply_add_fusion.1
  2.9 0.7 pad_add_fusion
  3.9 0.7 copy.57
  4.6 5.7 %all-to-all-start = ((s32[8,2,10]{2,1,0:T(2,128)}), s32[8,2,10]{2,1,0:T(2,128)S(1)}, u32[]{:S(2)}, u32[]{:S(2)}) async-start(s32[8,2,10]{2,1,0:T(2,128)} %bitcast.5), calls=%async_computation | async-start | bytes 16384 | tf_op jit(solution)/shard_map/all_to_all | solution.py:691
  10.3 0.7 and_select_fusion
  11.0 0.7 copy.68
  11.7 0.8 compare_reduce_fusion
  12.6 0.7 pad_maximum_fusion.5
  14.2 0.7 add_convert_fusion
  15.1 0.6 broadcast_bitcast_fusion.refs_6_
  15.7 1.3 pad_maximum_fusion.3.refs_13_
  17.0 1.3 pad_maximum_fusion.2.refs_14_
  18.7 1.2 pad_maximum_fusion.4.refs_0_
  19.9 0.7 broadcast_in_dim.110
  20.6 0.7 broadcast_in_dim_reshape.3.refs_7_
  21.3 0.7 copy.62.refs_9_
  22.0 0.6 convert_element_type.29.refs_10_
  22.6 1.5 copy.60.refs_2_
  24.2 1.0 copy.64.refs_12_
  25.2 1.0 copy.63.refs_11_
  27.0 0.6 reshape.250.refs_1_
  27.6 0.6 broadcast_in_dim.109
  28.3 148.4 %whole_layer.1 = (bf16[528,256]{1,0:T(8,128)(2,1)}, bf16[528,256]{1,0:T(8,128)(2,1)}, bf16[528,256]{1,0:T(8,128)(2,1)}, bf16[8,2,2,128,256]{4,3,2,1,0:T(8,128)(2,1)}) custom-call(f32[2,4]{1,0:T(2,128)} %pad_maximum_fusion.4.refs_0_, s32[16]{0:T(128)} %reshape.250.refs_1_, s32[512,1]{1,0:T(8,128)} %copy.60.refs_2_, s32[1,512]{1,0:T(1,128)} %refs_3_.1, ...), custom_call_target="tpu_custom_call" | custom-call | tf_op jit(solution)/shard_map/whole_layer/pallas_call | solution.py:610
  176.7 1.0 slice.39
  177.6 0.7 slice_bitcast_fusion
  178.4 1.0 slice.40
  179.4 2.3 %gather_fusion = bf16[16,2,128,256]{3,2,1,0:T(8,128)(2,1)S(1)} fusion(bf16[16,2,128,256]{3,2,1,0:T(8,128)(2,1)} %bitcast.44, s32[1024]{0:T(1024)S(1)} %pad_clamp_fusion), kind=kCustom, calls=%fused_computation | custom fusion | bytes 4194368 | tf_op jit(solution)/shard_map/gather | solution.py:765
  181.6 0.8 pad_maximum_fusion
  182.5 1.5 broadcast_select_fusion
  184.0 0.7 copy.75
  (35 shorter events, 2.8 us)
Async XLA Ops:
  4.6 21.7 %all-to-all-start = ((s32[8,2,10]{2,1,0:T(2,128)}), s32[8,2,10]{2,1,0:T(2,128)S(1)}, u32[]{:S(2)}, u32[]{:S(2)}) async-start(s32[8,2,10]{2,1,0:T(2,128)} %bitcast.5), calls=%async_computation | async-start | bytes 16384 | tf_op jit(solution)/shard_map/all_to_all | solution.py:691
  182.5 1.5 copy-start
